TPU v7x, 128 devices: a whole 4x4x4 slice. The times are simulated.
128 devices in a mesh: facet: 32 (over z, x_hi, y), vis: 4 (over x_lo, core).
Axes of the slice: x: 4 (x_hi: 2, x_lo: 2; x = x_hi * 2 + x_lo), y: 4, z: 4, core: 2. Of those that a mesh axis runs over, the one named last changes fastest.
Arguments:
- facet_image: float32 [2, 32768, 1024], P(None, ('facet', 'vis')), may hold values from -0.005859375 to 0.005859375
- contributions: int32 [4, 32, 8], P(None, 'facet'), may hold values from 0 to 31, as said below
- counts: int32 [4, 32], P('vis', 'facet'), may hold values from 1 to 512, as said below
- wplanes: int32 [4, 32, 512], P('vis', 'facet'), may hold values from 0 to 7
- kernel_offsets: int32 [2, 4, 32, 512, 128], P(None, 'vis', 'facet'), may hold values from 0 to 56
- kernel_frac: float32 [2, 4, 32, 512, 128], P(None, 'vis', 'facet'), may hold values from 0 to 1
- owners: int32 [4, 32, 512, 1], P('vis', 'facet'), may hold values from 0 to 3; in each aligned block of 512 rows (0 to 511, 512 to 1023, ..., all dimensions but the last counted through in order) at most 256 rows name the same one
Outputs:
- owned: float32 [4, 32, 4, 256, 256], P('vis', 'facet')
Inputs may be any that keep to these rules, and one draw needn't show every extreme that they name: For each column c, the lists contributions[r, c] of its 4 subgrids together name every facet exactly once. `counts`: subgrid (0, 0) has all 512 rows live. `owners`: the rows of one subgrid name one owner at most 256 times, and some subgrid names an owner exactly 256 times.
All inputs are finite; a program needn't handle non-finite values.
Results may differ from a plain program's by a relative error of at most 0.0003.
Values sent between devices are 32-bit elements; how exact they have to be, the bound alone decides.
No kernel may reach another device: no remote copies, remote signals or barrier semaphores. Data moves between devices by JAX's collectives and lax.ppermute only.
A program may use at most 64 MiB of HBM per device.

v0:
```python
import functools
import math

import jax
import jax.numpy as jnp
import ml_dtypes
import numpy as np
from jax import lax
from jax.experimental import pallas as pl
from jax.experimental.pallas import tpu as pltpu
from jax.sharding import PartitionSpec as P

FP = 1024
SUB = 64
CH = 128
NW = 8
USTEP = 129
VSTEP = 33
ROWS = 512
K = 8
NCOL = 32
CAP = 256
N_FACET = 32
N_VIS = 4
MOD = FP * N_FACET
XROWS = FP // N_VIS
YBLK = 256
NY = FP // YBLK

F32 = jnp.float32
BF16 = jnp.bfloat16
HIGHEST = lax.Precision.HIGHEST
VMEM_LIMIT = 56 * 1024 * 1024


def turns(first, second, modulus):
    return 2.0 * math.pi * ((first * second) % modulus) / modulus


def split_np(values):
    high = values.astype(ml_dtypes.bfloat16)
    low = (values - high.astype(np.float64)).astype(ml_dtypes.bfloat16)
    return high, low


@functools.cache
def tables():
    freq = USTEP * np.arange(N_VIS * SUB, dtype=np.int64)
    theta = turns(freq[:, None], np.arange(XROWS, dtype=np.int64)[None, :], MOD).reshape(N_VIS, SUB, XROWS)
    ch, cl = split_np(np.cos(theta))
    sh, sl = split_np(np.sin(theta))
    xtab = np.concatenate([ch, sh, cl, sl], 1)

    xrot = np.zeros((N_FACET * N_VIS, 8, N_VIS * SUB), np.float32)
    for f in range(N_FACET):
        for v in range(N_VIS):
            order = row_order(v // 2, v % 2)
            rows = np.concatenate([freq[r * SUB : (r + 1) * SUB] for r in order])
            angle = turns(rows, f * FP + v * XROWS, MOD)
            xrot[f * N_VIS + v, 0] = np.cos(angle)
            xrot[f * N_VIS + v, 1] = np.sin(angle)

    m = np.arange(NCOL * SUB, dtype=np.int64)
    theta = turns(np.arange(YBLK, dtype=np.int64)[:, None], VSTEP * m[None, :], MOD).reshape(YBLK, NCOL // 2, 128)
    ytab = np.concatenate([np.cos(theta), np.sin(theta)], -1).reshape(YBLK, NCOL // 2 * 256)
    ytab = np.stack(split_np(ytab))

    angle = turns(np.arange(NY, dtype=np.int64)[:, None] * YBLK, VSTEP * m[None, :], MOD)
    yrot = np.zeros((8, NCOL * SUB), np.float32)
    yrot[0:4] = np.cos(angle)
    yrot[4:8] = np.sin(angle)

    cells = np.arange(SUB, dtype=np.int64) - SUB // 2
    radius = cells[:, None] ** 2 + cells[None, :] ** 2
    theta = turns(np.arange(NW, dtype=np.int64)[:, None, None], radius[None], SUB * SUB)
    theta = theta.transpose(1, 0, 2).reshape(SUB, NW * SUB)
    screens = np.stack([np.cos(theta), np.sin(theta)]).astype(np.float32)

    index = np.arange(SUB, dtype=np.int64)
    angle = turns(index[:, None], index[None, :], SUB)
    dcos, dsin = np.cos(angle) / 16.0, np.sin(angle) / 16.0
    left = np.block([[dcos, dsin], [-dsin, dcos]]).astype(np.float32)
    zero = np.zeros_like(dcos)
    right = np.block([[dcos, zero, dsin, zero], [zero, dcos, zero, dsin]]).astype(np.float32)
    return xtab, xrot, ytab, yrot, screens, left, right


def row_order(x_lo, core):
    return [2 * (1 - x_lo) + 1 - core, 2 * x_lo + 1 - core, 2 * (1 - x_lo) + core, 2 * x_lo + core]


def split(values):
    high = values.astype(BF16)
    return high, (values - high.astype(F32)).astype(BF16)


def dot(a, b):
    return jnp.dot(a, b, preferred_element_type=F32)


def x_kernel(facet_ref, xtab_ref, xrot_ref, s0_ref, s1_ref, k0_ref, k1_ref, rot_ref):
    vis = lax.axis_index("vis")
    x_lo, core = vis // 2, vis % 2

    @pl.when(pl.program_id(0) == 0)
    def _():
        rot_ref[...] = xrot_ref[lax.axis_index("facet") * N_VIS + vis].T

    rhs = [split(facet_ref[0]), split(facet_ref[1])]
    order = row_order(x_lo, core)
    full = jnp.concatenate([xtab_ref[r] for r in order], 0)
    high = jnp.concatenate([xtab_ref[r, : 2 * SUB] for r in order], 0)
    a = []
    for hi, lo in rhs:
        both = dot(full, hi).reshape(N_VIS, 2, 2 * SUB, YBLK)
        a.append(both[:, 0] + both[:, 1] + dot(high, lo).reshape(N_VIS, 2 * SUB, YBLK))
    for i, out in enumerate((s0_ref, s1_ref, k0_ref, k1_ref)):
        re = a[0][i, :SUB] + a[1][i, SUB:]
        im = a[1][i, :SUB] - a[0][i, SUB:]
        cosine = rot_ref[i * SUB : (i + 1) * SUB, 0:1]
        sine = rot_ref[i * SUB : (i + 1) * SUB, 1:2]
        out[:SUB] = re * cosine + im * sine
        out[SUB:] = im * cosine - re * sine


def x_sum(facet_image, xtab, xrot):
    out = jax.ShapeDtypeStruct((2 * SUB, FP), F32)
    block = pl.BlockSpec((2 * SUB, YBLK), lambda i: (0, i))
    return pl.pallas_call(
        x_kernel,
        grid=(NY,),
        in_specs=[
            pl.BlockSpec((2, XROWS, YBLK), lambda i: (0, 0, i)),
            pl.BlockSpec(xtab.shape, lambda i: (0, 0, 0)),
            pl.BlockSpec(xrot.shape, lambda i: (0, 0, 0)),
        ],
        out_specs=[block] * 4,
        out_shape=[out] * 4,
        scratch_shapes=[pltpu.VMEM((N_VIS * SUB, 8), F32)],
        compiler_params=pltpu.CompilerParams(vmem_limit_bytes=VMEM_LIMIT),
        name="x_sum",
    )(facet_image, xtab, xrot)


def y_kernel(kept_ref, near_ref, far_ref, ytab_ref, yrot_ref, out_ref, lhs_ref):
    @pl.when(pl.program_id(0) == 0)
    def _():
        total = kept_ref[...] + near_ref[...] + far_ref[...]
        hi, lo = split(total)
        for y in range(NY):
            lhs_ref[y * 128 : (y + 1) * 128] = hi[:, y * YBLK : (y + 1) * YBLK]
            lhs_ref[NY * 128 + y * 128 : NY * 128 + (y + 1) * 128] = lo[:, y * YBLK : (y + 1) * YBLK]

    half = NY * 128
    both = dot(lhs_ref[...], ytab_ref[0])
    part = both[:half] + both[half:] + dot(lhs_ref[:half], ytab_ref[1])
    re = part[0:64, :128] + part[64:128, 128:]
    im = part[64:128, :128] - part[0:64, 128:]
    for y in range(1, NY):
        now = part[y * 128 : (y + 1) * 128]
        gre = now[0:64, :128] + now[64:128, 128:]
        gim = now[64:128, :128] - now[0:64, 128:]
        cosine = yrot_ref[y : y + 1]
        sine = yrot_ref[4 + y : 5 + y]
        re = re + gre * cosine + gim * sine
        im = im + gim * cosine - gre * sine
    first = lax.broadcasted_iota(jnp.int32, (64, 128), 1) < 64
    out_ref[0] = jnp.where(first, re, pltpu.roll(im, 64, 1))
    out_ref[1] = jnp.where(first, pltpu.roll(re, 64, 1), im)


def y_sum(kept, near, far, ytab, yrot):
    whole = pl.BlockSpec((2 * SUB, FP), lambda i: (0, 0))
    return pl.pallas_call(
        y_kernel,
        grid=(NCOL // 2,),
        in_specs=[
            whole,
            whole,
            whole,
            pl.BlockSpec((2, YBLK, 256), lambda i: (0, 0, i)),
            pl.BlockSpec((8, 128), lambda i: (0, i)),
        ],
        out_specs=pl.BlockSpec((2, SUB, 2 * SUB), lambda i: (i, 0, 0)),
        out_shape=jax.ShapeDtypeStruct((NCOL, SUB, 2 * SUB), F32),
        scratch_shapes=[pltpu.VMEM((2 * NY * 128, YBLK), BF16)],
        compiler_params=pltpu.CompilerParams(vmem_limit_bytes=VMEM_LIMIT),
        name="y_sum",
    )(kept, near, far, ytab, yrot)


TAPER = math.sqrt(0.5 * math.log2(math.e)) / 1.6


def degrid_kernel(
    lists_ref, counts_ref, wplanes_ref, owners_ref,
    blocks_ref, screens_ref, left_ref, right_ref, offsets_ref, frac_ref,
    out_ref, planes_ref, rows_ref, fill_ref,
):
    vis = lax.axis_index("vis")
    grid = blocks_ref[lists_ref[vis, 0]]
    for k in range(1, K):
        grid = grid + blocks_ref[lists_ref[vis, k]]
    turned = grid.T
    gre = jnp.concatenate([turned[:SUB]] * NW, 1)
    gim = jnp.concatenate([turned[SUB:]] * NW, 1)
    hre = gre * screens_ref[0] - gim * screens_ref[1]
    him = gre * screens_ref[1] + gim * screens_ref[0]
    along = jnp.dot(left_ref[...], jnp.concatenate([hre, him], 0), precision=HIGHEST, preferred_element_type=F32)
    first = lax.broadcasted_iota(jnp.int32, (128, 128), 1) < 64
    for pair in range(NW // 2):
        m = jnp.dot(along[:, pair * 128 : (pair + 1) * 128], right_ref[...], precision=HIGHEST, preferred_element_type=F32)
        re = m[:SUB, :128] + m[SUB:, 128:]
        im = m[SUB:, :128] - m[:SUB, 128:]
        both = jnp.concatenate([re, im], 0)
        swapped = pltpu.roll(both, 64, 1)
        for j, twice in enumerate((jnp.where(first, both, swapped), jnp.where(first, swapped, both))):
            hi, lo = split(twice)
            planes_ref[2 * pair + j, :, :128] = hi
            planes_ref[2 * pair + j, :, 128:] = lo

    rows_ref[...] = jnp.zeros_like(rows_ref)
    for o in range(N_VIS):
        fill_ref[o] = 0
    cell = lax.broadcasted_iota(jnp.int32, (8, CH), 0)
    count = counts_ref[0, 0]

    def taps(offset, frac):
        offset = jnp.broadcast_to(offset, (8, CH))
        shift = jnp.broadcast_to(frac, (8, CH))
        step = ((cell - offset) & 7).astype(F32)
        d = step * TAPER - shift
        value = jnp.exp2(-(d * d))
        return value, (offset - cell + 7) >> 3

    def body(group, carry):
        base = pl.multiple_of(group * 8, 8)
        ou = offsets_ref[0, 0, 0, pl.ds(base, 8), :]
        ov = offsets_ref[1, 0, 0, pl.ds(base, 8), :]
        fu = (frac_ref[0, 0, 0, pl.ds(base, 8), :] + 3.5) * TAPER
        fv = (frac_ref[1, 0, 0, pl.ds(base, 8), :] + 3.5) * TAPER
        for i in range(8):
            n = base + i
            uval, ublock = taps(ou[i : i + 1], fu[i : i + 1])
            vval, vblock = taps(ov[i : i + 1], fv[i : i + 1])
            uhi = uval.astype(BF16).astype(F32)
            ulo = uval - uhi
            zero = jnp.zeros_like(uhi)
            high = jnp.concatenate([jnp.where(ublock == j, uhi, zero) for j in range(8)], 0).astype(BF16)
            low = jnp.concatenate([jnp.where(ublock == j, ulo, zero) for j in range(8)], 0).astype(BF16)
            t = dot(planes_ref[wplanes_ref[0, 0, n], :, :192], jnp.concatenate([high, low, high], 0))
            are, aim = t[0:8], t[64:72]
            for j in range(1, 8):
                here = vblock == j
                are = jnp.where(here, t[8 * j : 8 * j + 8], are)
                aim = jnp.where(here, t[64 + 8 * j : 72 + 8 * j], aim)
            live = jnp.where(n < count, 1.0, 0.0)
            re = jnp.sum(are * vval, 0, keepdims=True) * live
            im = jnp.sum(aim * vval, 0, keepdims=True) * live
            owner = owners_ref[0, 0, n]
            slot = fill_ref[owner]
            fill_ref[owner] = slot + 1
            place = owner * (2 * CAP) + slot + (slot & ~7)
            rows_ref[pl.ds(place, 1), :] = re
            rows_ref[pl.ds(place + 8, 1), :] = im
        return carry

    lax.fori_loop(0, ROWS // 8, body, 0)

    tiles = rows_ref[...].reshape(N_VIS, CAP // 8, 2, 8, CH)
    out_ref[:, :, :CH] = tiles[:, :, 0].reshape(N_VIS, CAP, CH)
    out_ref[:, :, CH:] = tiles[:, :, 1].reshape(N_VIS, CAP, CH)


def degrid(lists, counts, wplanes, owners, blocks, screens, left, right, offsets, frac):
    smem = pl.BlockSpec(memory_space=pltpu.SMEM)
    vmem = pl.BlockSpec(memory_space=pltpu.VMEM)
    return pl.pallas_call(
        degrid_kernel,
        in_specs=[smem] * 4 + [vmem] * 6,
        out_specs=vmem,
        out_shape=jax.ShapeDtypeStruct((N_VIS, CAP, 2 * CH), F32),
        scratch_shapes=[pltpu.VMEM((NW, 128, 256), BF16), pltpu.VMEM((2 * N_VIS * CAP, CH), F32), pltpu.SMEM((N_VIS,), jnp.int32)],
        compiler_params=pltpu.CompilerParams(vmem_limit_bytes=VMEM_LIMIT),
        name="degrid",
    )(lists, counts, wplanes, owners, blocks, screens, left, right, offsets, frac)


TO_CORE = [(0, 1), (1, 0), (2, 3), (3, 2)]
TO_CHIP = [(0, 2), (2, 0), (1, 3), (3, 1)]


def on_device(facet_image, contributions, counts, wplanes, kernel_offsets, kernel_frac, owners):
    xtab, xrot, ytab, yrot, screens, left, right = [jnp.asarray(t) for t in tables()]
    s0, s1, k0, k1 = x_sum(facet_image, xtab, xrot)
    r0 = lax.ppermute(s0, "vis", TO_CORE)
    r1 = lax.ppermute(s1, "vis", TO_CORE)
    far = lax.ppermute(k0 + r0, "vis", TO_CHIP)
    blocks = y_sum(k1, r1, far, ytab, yrot)
    arrived = lax.all_to_all(blocks, "facet", split_axis=0, concat_axis=0, tiled=True)
    outgoing = degrid(
        contributions[:, 0, :], counts, wplanes, owners[..., 0], arrived, screens, left, right, kernel_offsets, kernel_frac
    )
    owned = lax.all_to_all(outgoing, "vis", split_axis=0, concat_axis=0, tiled=True)
    return owned.reshape(1, 1, N_VIS, CAP, 2 * CH)


def solution(mesh):
    return jax.shard_map(
        on_device,
        mesh=mesh,
        in_specs=(
            P(None, ("facet", "vis"), None),
            P(None, "facet", None),
            P("vis", "facet"),
            P("vis", "facet", None),
            P(None, "vis", "facet", None, None),
            P(None, "vis", "facet", None, None),
            P("vis", "facet", None, None),
        ),
        out_specs=P("vis", "facet", None, None, None),
        check_vma=False,
    )
```

profile of v0, /device:TPU:1, one launch (start us, length us, event | category | flops | bytes accessed | tf_op | source)
XLA Modules:
  0.0 109.8 jit_solution(16265263445282376042)
XLA Ops:
  0.0 5.4 %x_sum.1 = (f32[128,1024]{1,0:T(8,128)}, f32[128,1024]{1,0:T(8,128)}, f32[128,1024]{1,0:T(8,128)}, f32[128,1024]{1,0:T(8,128)}) custom-call(f32[2,256,1024]{2,1,0:T(8,128)} %facet_ref.1, bf16[4,256,256]{2,1,0:T(8,128)(2,1)} %constant.14.clone.xtab_ref, f32[128,8,256]{2,1,0:T(8,128)} %constant.15.clone.xrot_ref), custom_call_target="tpu_custom_call" | custom-call | tf_op jit(solution)/shard_map/x_sum/pallas_call | solution.py:129
  5.4 1.4 %collective-permute-start.1 = (f32[128,1024]{1,0:T(8,128)}, f32[128,1024]{1,0:T(8,128)S(1)}, u32[]{:S(2)}, u32[]{:S(2)}) collective-permute-start(f32[128,1024]{1,0:T(8,128)} %get-tuple-element.12), channel_id=1, source_target_pairs={{0,1},{1,0},{2,3},{3,2},{4,5},{5,4},{6,7},{7,6},{8,9},{9,8},{10,11... | collective-permute-start | bytes 1572872 | tf_op jit(solution)/shard_map/ppermute | solution.py:296
  6.8 0.1 collective-permute-start
  6.9 1.7 %collective-permute-done.1 = f32[128,1024]{1,0:T(8,128)S(1)} collective-permute-done((f32[128,1024]{1,0:T(8,128)}, f32[128,1024]{1,0:T(8,128)S(1)}, u32[]{:S(2)}, u32[]{:S(2)}) %collective-permute-start.1) | collective-permute-done | bytes 524320 | tf_op jit(solution)/shard_map/ppermute | solution.py:296
  8.6 1.1 %add.3 = f32[128,1024]{1,0:T(8,128)S(1)} add(f32[128,1024]{1,0:T(8,128)} %get-tuple-element.11, f32[128,1024]{1,0:T(8,128)S(1)} %collective-permute-done.1) | non-fusion elementwise | flops 131072 | bytes 1572864 | tf_op jit(solution)/shard_map/add | solution.py:298
  9.7 1.4 %collective-permute-start.2 = (f32[128,1024]{1,0:T(8,128)S(1)}, f32[128,1024]{1,0:T(8,128)S(1)}, u32[]{:S(2)}, u32[]{:S(2)}) collective-permute-start(f32[128,1024]{1,0:T(8,128)S(1)} %add.3), channel_id=1, source_target_pairs={{0,2},{2,0},{1,3},{3,1},{4,6},{6,4},{5,7},{7,5},{8,10},{10,8},{9,1... | collective-permute-start | bytes 1572872 | tf_op jit(solution)/shard_map/ppermute | solution.py:298
  11.1 0.0 collective-permute-done.near_ref
  11.1 0.0 copy-start.1
  11.1 11.8 %collective-permute-done.2.far_ref = f32[128,1024]{1,0:T(8,128)S(1)} collective-permute-done((f32[128,1024]{1,0:T(8,128)S(1)}, f32[128,1024]{1,0:T(8,128)S(1)}, u32[]{:S(2)}, u32[]{:S(2)}) %collective-permute-start.2) | collective-permute-done | bytes 524320 | tf_op jit(solution)/shard_map/ppermute | solution.py:298
  22.9 0.0 copy-start.2
  22.9 0.0 copy-done.1
  22.9 0.8 copy-done.2
  23.7 13.5 %y_sum.1 = f32[32,64,128]{2,1,0:T(8,128)} custom-call(f32[128,1024]{1,0:T(8,128)} %get-tuple-element.9.kept_ref, f32[128,1024]{1,0:T(8,128)} %copy-done.1, f32[128,1024]{1,0:T(8,128)} %copy-done.2, bf16[2,256,4096]{2,1,0:T(8,128)(2,1)} %constant.16.clone.ytab_ref, f32[8,2048]{1,0:T(8,128)} %constant.17.clone.yrot_ref), custom_call_target="tpu_custom_call" | custom-call | tf_op jit(solution)/shard_map/y_sum/pallas_call | solution.py:174
  37.2 10.6 %all-to-all-start = ((f32[32,64,128]{2,1,0:T(8,128)}), f32[32,64,128]{2,1,0:T(8,128)S(1)}, u32[]{:S(2)}, u32[]{:S(2)}) async-start(f32[32,64,128]{2,1,0:T(8,128)} %y_sum.1), calls=%async_computation | async-start | bytes 2097152 | tf_op jit(solution)/shard_map/all_to_all | solution.py:300
  48.4 15.6 %all-to-all-done.blocks_ref = f32[32,64,128]{2,1,0:T(8,128)S(1)} async-done(((f32[32,64,128]{2,1,0:T(8,128)}), f32[32,64,128]{2,1,0:T(8,128)S(1)}, u32[]{:S(2)}, u32[]{:S(2)}) %all-to-all-start) | async-done | bytes 1048608 | tf_op jit(solution)/shard_map/all_to_all | solution.py:300
  64.1 0.0 copy-start
  64.1 1.0 copy-done
  65.0 24.4 %degrid.1 = f32[4,256,256]{2,1,0:T(8,128)} custom-call(s32[4,8]{1,0:T(4,128)} %bitcast.4, s32[1,1]{1,0:T(1,128)S(6)} %copy.16.counts_ref, s32[1,1,512]{2,1,0:T(1,128)} %wplanes_ref.1, s32[1,1,512]{2,1,0:T(1,128)} %bitcast.5, f32[32,64,128]{2,1,0:T(8,128)} %copy-done, f32[2,64,512]{2,1,0:T(8,128)} %constant.18.clone.screens_ref, ...), custom_call_target="tpu_custom_call" | custom-call | tf_op jit(solution)/shard_map/degrid/pallas_call | solution.py:278
  89.5 19.4 %all_to_all.10 = f32[4,256,256]{2,1,0:T(8,128)S(1)} all-to-all(f32[4,256,256]{2,1,0:T(8,128)} %degrid.1), channel_id=1, replica_groups=mesh['facet'=32,'vis'=4] {'vis'}, dimensions={0} | all-to-all | bytes 2097152 | tf_op jit(solution)/shard_map/all_to_all | solution.py:304
  108.9 1.0 copy.17
Async XLA Ops:
  5.4 3.2 %collective-permute-start.1 = (f32[128,1024]{1,0:T(8,128)}, f32[128,1024]{1,0:T(8,128)S(1)}, u32[]{:S(2)}, u32[]{:S(2)}) collective-permute-start(f32[128,1024]{1,0:T(8,128)} %get-tuple-element.12), channel_id=1, source_target_pairs={{0,1},{1,0},{2,3},{3,2},{4,5},{5,4},{6,7},{7,6},{8,9},{9,8},{10,11... | collective-permute-start | bytes 1572872 | tf_op jit(solution)/shard_map/ppermute | solution.py:296
  6.8 4.3 %collective-permute-start = (f32[128,1024]{1,0:T(8,128)}, f32[128,1024]{1,0:T(8,128)S(1)}, u32[]{:S(2)}, u32[]{:S(2)}) collective-permute-start(f32[128,1024]{1,0:T(8,128)} %get-tuple-element.10), channel_id=1, source_target_pairs={{0,1},{1,0},{2,3},{3,2},{4,5},{5,4},{6,7},{7,6},{8,9},{9,8},{10,11... | collective-permute-start | bytes 1572872 | tf_op jit(solution)/shard_map/ppermute | solution.py:297
  9.7 13.2 %collective-permute-start.2 = (f32[128,1024]{1,0:T(8,128)S(1)}, f32[128,1024]{1,0:T(8,128)S(1)}, u32[]{:S(2)}, u32[]{:S(2)}) collective-permute-start(f32[128,1024]{1,0:T(8,128)S(1)} %add.3), channel_id=1, source_target_pairs={{0,2},{2,0},{1,3},{3,1},{4,6},{6,4},{5,7},{7,5},{8,10},{10,8},{9,1... | collective-permute-start | bytes 1572872 | tf_op jit(solution)/shard_map/ppermute | solution.py:298
  11.1 11.8 %copy-start.1 = (f32[128,1024]{1,0:T(8,128)}, f32[128,1024]{1,0:T(8,128)S(1)}, u32[]{:S(2)}) copy-start(f32[128,1024]{1,0:T(8,128)S(1)} %collective-permute-done.near_ref) | copy-start | bytes 1572868
  22.9 0.8 copy-start.2
  37.2 26.9 %all-to-all-start = ((f32[32,64,128]{2,1,0:T(8,128)}), f32[32,64,128]{2,1,0:T(8,128)S(1)}, u32[]{:S(2)}, u32[]{:S(2)}) async-start(f32[32,64,128]{2,1,0:T(8,128)} %y_sum.1), calls=%async_computation | async-start | bytes 2097152 | tf_op jit(solution)/shard_map/all_to_all | solution.py:300
  64.1 1.0 copy-start
where the time goes:
time: 111 us; the launch traced here: 110 us
  Pallas kernels  43.3 us (39%)
  waiting for transfers between devices  29.1 us (26%)
  blocking collectives  19.4 us (17%)
  starting transfers between devices  13.5 us (12%)
  local copies, waits for them, and re-layouts  2.75 us (2%)
  other arithmetic  1.12 us (1%)
    pallas_call x1, Pallas kernels, degrid(): pl.pallas_call(degrid_kernel, in_specs=[smem] * 4 + [vmem] * 6, out_specs...  24.4 us
    all_to_all x1, blocking collectives, on_device(): lax.all_to_all(outgoing, 'vis', split_axis=0, concat_axis=0, tiled=True)  19.4 us
    all_to_all x1, waiting for transfers between devices, on_device(): lax.all_to_all(blocks, 'facet', split_axis=0, concat_axis=0, tiled=True)  15.6 us
    pallas_call x1, Pallas kernels, y_sum(): pl.pallas_call(y_kernel, grid=(NCOL // 2,), in_specs=[whole, whole, whole...  13.5 us
    ppermute x1, waiting for transfers between devices, on_device(): far = lax.ppermute(k0 + r0, 'vis', TO_CHIP)  11.8 us
    all_to_all x1, starting transfers between devices, on_device(): lax.all_to_all(blocks, 'facet', split_axis=0, concat_axis=0, tiled=True)  10.6 us
    pallas_call x1, Pallas kernels, x_sum(): pl.pallas_call(x_kernel, grid=(NY,), in_specs=[pl.BlockSpec((2, XROWS, YB...  5.4 us
    unnamed x7, local copies, waits for them, and re-layouts  2.75 us
  transfers between devices with their start and end apart: 4, of which 3 were waited for; matrix products, arithmetic and copies ran while one was open for 1% of the time, Pallas kernels for 0%

commit v1 on v0

--- a/solution.py
+++ b/solution.py
@@ -30,7 +30,7 @@
 F32 = jnp.float32
 BF16 = jnp.bfloat16
 HIGHEST = lax.Precision.HIGHEST
-VMEM_LIMIT = 56 * 1024 * 1024
+VMEM_LIMIT = 20 * 1024 * 1024
 
 
 def turns(first, second, modulus):
@@ -62,8 +62,8 @@
 
     m = np.arange(NCOL * SUB, dtype=np.int64)
     theta = turns(np.arange(YBLK, dtype=np.int64)[:, None], VSTEP * m[None, :], MOD).reshape(YBLK, NCOL // 2, 128)
-    ytab = np.concatenate([np.cos(theta), np.sin(theta)], -1).reshape(YBLK, NCOL // 2 * 256)
-    ytab = np.stack(split_np(ytab))
+    ytab = np.concatenate([np.cos(theta), np.sin(theta)], -1).transpose(1, 0, 2)
+    ytab = np.stack(split_np(ytab), 1)
 
     angle = turns(np.arange(NY, dtype=np.int64)[:, None] * YBLK, VSTEP * m[None, :], MOD)
     yrot = np.zeros((8, NCOL * SUB), np.float32)
@@ -137,7 +137,7 @@
         out_specs=[block] * 4,
         out_shape=[out] * 4,
         scratch_shapes=[pltpu.VMEM((N_VIS * SUB, 8), F32)],
-        compiler_params=pltpu.CompilerParams(vmem_limit_bytes=VMEM_LIMIT),
+        compiler_params=pltpu.CompilerParams(vmem_limit_bytes=60 * 1024 * 1024),
         name="x_sum",
     )(facet_image, xtab, xrot)
 
@@ -152,36 +152,40 @@
             lhs_ref[NY * 128 + y * 128 : NY * 128 + (y + 1) * 128] = lo[:, y * YBLK : (y + 1) * YBLK]
 
     half = NY * 128
-    both = dot(lhs_ref[...], ytab_ref[0])
-    part = both[:half] + both[half:] + dot(lhs_ref[:half], ytab_ref[1])
-    re = part[0:64, :128] + part[64:128, 128:]
-    im = part[64:128, :128] - part[0:64, 128:]
-    for y in range(1, NY):
-        now = part[y * 128 : (y + 1) * 128]
-        gre = now[0:64, :128] + now[64:128, 128:]
-        gim = now[64:128, :128] - now[0:64, 128:]
-        cosine = yrot_ref[y : y + 1]
-        sine = yrot_ref[4 + y : 5 + y]
-        re = re + gre * cosine + gim * sine
-        im = im + gim * cosine - gre * sine
     first = lax.broadcasted_iota(jnp.int32, (64, 128), 1) < 64
-    out_ref[0] = jnp.where(first, re, pltpu.roll(im, 64, 1))
-    out_ref[1] = jnp.where(first, pltpu.roll(re, 64, 1), im)
+    lhs = jnp.concatenate([lhs_ref[:half], lhs_ref[half:], lhs_ref[:half]], 1)
+    for w in range(PAIRS):
+        part = dot(lhs, jnp.concatenate([ytab_ref[w, 0], ytab_ref[w, 0], ytab_ref[w, 1]], 0))
+        re = part[0:64, :128] + part[64:128, 128:]
+        im = part[64:128, :128] - part[0:64, 128:]
+        for y in range(1, NY):
+            now = part[y * 128 : (y + 1) * 128]
+            gre = now[0:64, :128] + now[64:128, 128:]
+            gim = now[64:128, :128] - now[0:64, 128:]
+            cosine = yrot_ref[y : y + 1, w * 128 : (w + 1) * 128]
+            sine = yrot_ref[4 + y : 5 + y, w * 128 : (w + 1) * 128]
+            re = re + gre * cosine + gim * sine
+            im = im + gim * cosine - gre * sine
+        out_ref[2 * w] = jnp.where(first, re, pltpu.roll(im, 64, 1))
+        out_ref[2 * w + 1] = jnp.where(first, pltpu.roll(re, 64, 1), im)
+
+
+PAIRS = 4
 
 
 def y_sum(kept, near, far, ytab, yrot):
     whole = pl.BlockSpec((2 * SUB, FP), lambda i: (0, 0))
     return pl.pallas_call(
         y_kernel,
-        grid=(NCOL // 2,),
+        grid=(NCOL // 2 // PAIRS,),
         in_specs=[
             whole,
             whole,
             whole,
-            pl.BlockSpec((2, YBLK, 256), lambda i: (0, 0, i)),
-            pl.BlockSpec((8, 128), lambda i: (0, i)),
+            pl.BlockSpec((PAIRS, 2, YBLK, 256), lambda i: (i, 0, 0, 0)),
+            pl.BlockSpec((8, 128 * PAIRS), lambda i: (0, i)),
         ],
-        out_specs=pl.BlockSpec((2, SUB, 2 * SUB), lambda i: (i, 0, 0)),
+        out_specs=pl.BlockSpec((2 * PAIRS, SUB, 2 * SUB), lambda i: (i, 0, 0)),
         out_shape=jax.ShapeDtypeStruct((NCOL, SUB, 2 * SUB), F32),
         scratch_shapes=[pltpu.VMEM((2 * NY * 128, YBLK), BF16)],
         compiler_params=pltpu.CompilerParams(vmem_limit_bytes=VMEM_LIMIT),
@@ -190,13 +194,75 @@
 
 
 TAPER = math.sqrt(0.5 * math.log2(math.e)) / 1.6
-
-
-def degrid_kernel(
-    lists_ref, counts_ref, wplanes_ref, owners_ref,
-    blocks_ref, screens_ref, left_ref, right_ref, offsets_ref, frac_ref,
-    out_ref, planes_ref, rows_ref, fill_ref,
-):
+STEP = 32
+SPAN = ROWS + 2 * NW + 2 * STEP
+JUNK = 2 * 2 * CAP
+
+
+def order_kernel(counts_ref, wplanes_ref, owners_ref, row_ref, place_ref, ends_ref, key_ref, fill_ref):
+    vis = lax.axis_index("vis")
+    count = counts_ref[0, 0]
+    for i in range(2 * NW):
+        key_ref[i] = 0
+    for i in range(N_VIS):
+        fill_ref[i] = 0
+
+    def clear(i, carry):
+        for j in range(8):
+            row_ref[i * 8 + j] = 0
+            place_ref[i * 8 + j] = JUNK
+        return carry
+
+    lax.fori_loop(0, SPAN // 8, clear, 0)
+
+    def tally(i, carry):
+        for j in range(8):
+            n = i * 8 + j
+            key = wplanes_ref[0, 0, n] + NW * (1 - ((owners_ref[0, 0, n] ^ vis) >> 1))
+            key_ref[key] = key_ref[key] + jnp.where(n < count, 1, 0)
+        return carry
+
+    lax.fori_loop(0, ROWS // 8, tally, 0)
+    start = jnp.int32(0)
+    for part in range(2):
+        for w in range(NW):
+            held = key_ref[part * NW + w]
+            key_ref[part * NW + w] = start
+            start = start + ((held + 1) & ~1)
+        start = (start + STEP - 1) & ~(STEP - 1)
+        ends_ref[part] = start // STEP
+
+    def deal(i, carry):
+        for j in range(8):
+            n = i * 8 + j
+            apart = owners_ref[0, 0, n] ^ vis
+            slot = fill_ref[apart]
+            fill_ref[apart] = slot + 1
+            key = wplanes_ref[0, 0, n] + NW * (1 - (apart >> 1))
+            at = jnp.where(n < count, key_ref[key], SPAN)
+            key_ref[key] = key_ref[key] + jnp.where(n < count, 1, 0)
+            row_ref[at] = n
+            place_ref[at] = (apart & 1) * (2 * CAP) + slot + (slot & ~7)
+        return carry
+
+    lax.fori_loop(0, ROWS // 8, deal, 0)
+
+
+def order_rows(counts, wplanes, owners):
+    smem = pl.BlockSpec(memory_space=pltpu.SMEM)
+    flat = jax.ShapeDtypeStruct((SPAN + 8,), jnp.int32)
+    return pl.pallas_call(
+        order_kernel,
+        in_specs=[smem] * 3,
+        out_specs=[smem] * 3,
+        out_shape=[flat, flat, jax.ShapeDtypeStruct((2,), jnp.int32)],
+        scratch_shapes=[pltpu.SMEM((2 * NW,), jnp.int32), pltpu.SMEM((N_VIS,), jnp.int32)],
+        cost_estimate=pl.CostEstimate(flops=20_000_000, bytes_accessed=20_000_000, transcendentals=0),
+        name="order_rows",
+    )(counts, wplanes, owners)
+
+
+def planes_kernel(lists_ref, blocks_ref, screens_ref, left_ref, right_ref, planes_ref):
     vis = lax.axis_index("vis")
     grid = blocks_ref[lists_ref[vis, 0]]
     for k in range(1, K):
@@ -219,75 +285,111 @@
             planes_ref[2 * pair + j, :, :128] = hi
             planes_ref[2 * pair + j, :, 128:] = lo
 
+
+def make_planes(lists, blocks, screens, left, right):
+    vmem = pl.BlockSpec(memory_space=pltpu.VMEM)
+    return pl.pallas_call(
+        planes_kernel,
+        in_specs=[pl.BlockSpec(memory_space=pltpu.SMEM)] + [vmem] * 4,
+        out_specs=vmem,
+        out_shape=jax.ShapeDtypeStruct((NW, 128, 256), BF16),
+        compiler_params=pltpu.CompilerParams(vmem_limit_bytes=VMEM_LIMIT),
+        name="make_planes",
+    )(lists, blocks, screens, left, right)
+
+
+def degrid_kernel(
+    row_ref, place_ref, ends_ref, wplanes_ref, planes_ref, offsets_ref, frac_ref, out0_ref, out1_ref, rows_ref, *, part
+):
     rows_ref[...] = jnp.zeros_like(rows_ref)
-    for o in range(N_VIS):
-        fill_ref[o] = 0
     cell = lax.broadcasted_iota(jnp.int32, (8, CH), 0)
-    count = counts_ref[0, 0]
-
-    def taps(offset, frac):
-        offset = jnp.broadcast_to(offset, (8, CH))
-        shift = jnp.broadcast_to(frac, (8, CH))
+    ahead = cell - 7
+
+    def taps(axis, n):
+        offset = jnp.broadcast_to(offsets_ref[axis, 0, 0, pl.ds(n, 1), :], (8, CH))
+        shift = (jnp.broadcast_to(frac_ref[axis, 0, 0, pl.ds(n, 1), :], (8, CH)) + 3.5) * TAPER
         step = ((cell - offset) & 7).astype(F32)
         d = step * TAPER - shift
-        value = jnp.exp2(-(d * d))
-        return value, (offset - cell + 7) >> 3
+        return jnp.exp2(-(d * d)), (offset - ahead) >> 3
 
     def body(group, carry):
-        base = pl.multiple_of(group * 8, 8)
-        ou = offsets_ref[0, 0, 0, pl.ds(base, 8), :]
-        ov = offsets_ref[1, 0, 0, pl.ds(base, 8), :]
-        fu = (frac_ref[0, 0, 0, pl.ds(base, 8), :] + 3.5) * TAPER
-        fv = (frac_ref[1, 0, 0, pl.ds(base, 8), :] + 3.5) * TAPER
-        for i in range(8):
-            n = base + i
-            uval, ublock = taps(ou[i : i + 1], fu[i : i + 1])
-            vval, vblock = taps(ov[i : i + 1], fv[i : i + 1])
-            uhi = uval.astype(BF16).astype(F32)
-            ulo = uval - uhi
-            zero = jnp.zeros_like(uhi)
-            high = jnp.concatenate([jnp.where(ublock == j, uhi, zero) for j in range(8)], 0).astype(BF16)
-            low = jnp.concatenate([jnp.where(ublock == j, ulo, zero) for j in range(8)], 0).astype(BF16)
-            t = dot(planes_ref[wplanes_ref[0, 0, n], :, :192], jnp.concatenate([high, low, high], 0))
-            are, aim = t[0:8], t[64:72]
-            for j in range(1, 8):
-                here = vblock == j
-                are = jnp.where(here, t[8 * j : 8 * j + 8], are)
-                aim = jnp.where(here, t[64 + 8 * j : 72 + 8 * j], aim)
-            live = jnp.where(n < count, 1.0, 0.0)
-            re = jnp.sum(are * vval, 0, keepdims=True) * live
-            im = jnp.sum(aim * vval, 0, keepdims=True) * live
-            owner = owners_ref[0, 0, n]
-            slot = fill_ref[owner]
-            fill_ref[owner] = slot + 1
-            place = owner * (2 * CAP) + slot + (slot & ~7)
-            rows_ref[pl.ds(place, 1), :] = re
-            rows_ref[pl.ds(place + 8, 1), :] = im
+        base = group * STEP
+        for i in range(0, STEP, 2):
+            pair = [row_ref[base + i], row_ref[base + i + 1]]
+            sides, high, low = [], [], []
+            for n in pair:
+                uval, ublock = taps(0, n)
+                uhi = uval.astype(BF16).astype(F32)
+                ulo = uval - uhi
+                zero = jnp.zeros_like(uhi)
+                high.append(jnp.concatenate([jnp.where(ublock == j, uhi, zero) for j in range(8)], 0).astype(BF16))
+                low.append(jnp.concatenate([jnp.where(ublock == j, ulo, zero) for j in range(8)], 0).astype(BF16))
+            high = jnp.concatenate(high, 1)
+            low = jnp.concatenate(low, 1)
+            both = dot(planes_ref[wplanes_ref[0, 0, pair[0]], :, :192], jnp.concatenate([high, low, high], 0))
+            for side, n in enumerate(pair):
+                t = both[:, side * CH : (side + 1) * CH]
+                vval, vblock = taps(1, n)
+                are, aim = t[0:8], t[64:72]
+                for j in range(1, 8):
+                    here = vblock == j
+                    are = jnp.where(here, t[8 * j : 8 * j + 8], are)
+                    aim = jnp.where(here, t[64 + 8 * j : 72 + 8 * j], aim)
+                place = place_ref[base + i + side]
+                rows_ref[pl.ds(place, 1), :] = jnp.sum(are * vval, 0, keepdims=True)
+                rows_ref[pl.ds(place + 8, 1), :] = jnp.sum(aim * vval, 0, keepdims=True)
         return carry
 
-    lax.fori_loop(0, ROWS // 8, body, 0)
-
-    tiles = rows_ref[...].reshape(N_VIS, CAP // 8, 2, 8, CH)
-    out_ref[:, :, :CH] = tiles[:, :, 0].reshape(N_VIS, CAP, CH)
-    out_ref[:, :, CH:] = tiles[:, :, 1].reshape(N_VIS, CAP, CH)
-
-
-def degrid(lists, counts, wplanes, owners, blocks, screens, left, right, offsets, frac):
+    lax.fori_loop(0 if part == 0 else ends_ref[0], ends_ref[part], body, 0)
+
+    for side, out in enumerate((out0_ref, out1_ref)):
+        tiles = rows_ref[side * 2 * CAP : (side + 1) * 2 * CAP].reshape(CAP // 8, 2, 8, CH)
+        out[:, :CH] = tiles[:, 0].reshape(CAP, CH)
+        out[:, CH:] = tiles[:, 1].reshape(CAP, CH)
+
+
+def degrid(part, row, place, ends, wplanes, planes, offsets, frac):
     smem = pl.BlockSpec(memory_space=pltpu.SMEM)
     vmem = pl.BlockSpec(memory_space=pltpu.VMEM)
-    return pl.pallas_call(
-        degrid_kernel,
-        in_specs=[smem] * 4 + [vmem] * 6,
-        out_specs=vmem,
-        out_shape=jax.ShapeDtypeStruct((N_VIS, CAP, 2 * CH), F32),
-        scratch_shapes=[pltpu.VMEM((NW, 128, 256), BF16), pltpu.VMEM((2 * N_VIS * CAP, CH), F32), pltpu.SMEM((N_VIS,), jnp.int32)],
+    out = jax.ShapeDtypeStruct((CAP, 2 * CH), F32)
+    return pl.pallas_call(
+        functools.partial(degrid_kernel, part=part),
+        in_specs=[smem] * 4 + [vmem] * 3,
+        out_specs=[vmem] * 2,
+        out_shape=[out] * 2,
+        scratch_shapes=[pltpu.VMEM((2 * 2 * CAP + 16, CH), F32)],
         compiler_params=pltpu.CompilerParams(vmem_limit_bytes=VMEM_LIMIT),
-        name="degrid",
-    )(lists, counts, wplanes, owners, blocks, screens, left, right, offsets, frac)
+        cost_estimate=pl.CostEstimate(flops=4_000_000_000, bytes_accessed=2_000_000, transcendentals=0),
+        name="degrid_" + ("far", "near")[part],
+    )(row, place, ends, wplanes, planes, offsets, frac)
+
+
+def gather_kernel(self_ref, core_ref, chip_ref, cross_ref, out_ref, sems):
+    vis = lax.axis_index("vis")
+    copies = [
+        pltpu.make_async_copy(ref, out_ref.at[0, 0, vis ^ i], sems.at[i])
+        for i, ref in enumerate((self_ref, core_ref, chip_ref, cross_ref))
+    ]
+    for copy in copies:
+        copy.start()
+    for copy in copies:
+        copy.wait()
+
+
+def gather_rows(*blocks):
+    return pl.pallas_call(
+        gather_kernel,
+        in_specs=[pl.BlockSpec(memory_space=pltpu.VMEM)] * N_VIS,
+        out_specs=pl.BlockSpec(memory_space=pl.ANY),
+        out_shape=jax.ShapeDtypeStruct((1, 1, N_VIS, CAP, 2 * CH), F32),
+        scratch_shapes=[pltpu.SemaphoreType.DMA((N_VIS,))],
+        name="gather_rows",
+    )(*blocks)
 
 
 TO_CORE = [(0, 1), (1, 0), (2, 3), (3, 2)]
 TO_CHIP = [(0, 2), (2, 0), (1, 3), (3, 1)]
+TO_CROSS = [(0, 3), (3, 0), (1, 2), (2, 1)]
 
 
 def on_device(facet_image, contributions, counts, wplanes, kernel_offsets, kernel_frac, owners):
@@ -297,12 +399,15 @@
     r1 = lax.ppermute(s1, "vis", TO_CORE)
     far = lax.ppermute(k0 + r0, "vis", TO_CHIP)
     blocks = y_sum(k1, r1, far, ytab, yrot)
+    row, place, ends = order_rows(counts, wplanes, owners[..., 0])
     arrived = lax.all_to_all(blocks, "facet", split_axis=0, concat_axis=0, tiled=True)
-    outgoing = degrid(
-        contributions[:, 0, :], counts, wplanes, owners[..., 0], arrived, screens, left, right, kernel_offsets, kernel_frac
-    )
-    owned = lax.all_to_all(outgoing, "vis", split_axis=0, concat_axis=0, tiled=True)
-    return owned.reshape(1, 1, N_VIS, CAP, 2 * CH)
+    planes = make_planes(contributions[:, 0, :], arrived, screens, left, right)
+    to_chip, to_cross = degrid(0, row, place, ends, wplanes, planes, kernel_offsets, kernel_frac)
+    from_chip = lax.ppermute(to_chip, "vis", TO_CHIP)
+    from_cross = lax.ppermute(to_cross, "vis", TO_CROSS)
+    own, to_core = degrid(1, row, place, ends, wplanes, planes, kernel_offsets, kernel_frac)
+    from_core = lax.ppermute(to_core, "vis", TO_CORE)
+    return gather_rows(own, from_core, from_chip, from_cross)
 
 
 def solution(mesh):

time: 111 us -> 89.6 us (0.81)
  blocking collectives: 19.4 us -> 0 us
  Pallas kernels: 43.3 us -> 32.9 us
  starting transfers between devices: 13.5 us -> 18.6 us
  local copies, waits for them, and re-layouts: 2.75 us -> 6.76 us
    all_to_all x1 -> x0, blocking collectives: 19.4 us -> none  [on_device(): lax.all_to_all(outgoing, 'vis', split_axis=0, concat_axis=0, tiled=True)]
    pallas_call x2 -> x6, Pallas kernels: 37.9 us -> 27.6 us  [the longest x1 9.52 us: order_rows(): pl.pallas_call(order_kernel, in_specs=[smem] * 3, out_specs=[smem] * 3, o...]
    all_to_all x1, waiting for transfers between devices: 15.6 us -> 6.12 us  [on_device(): lax.all_to_all(blocks, 'facet', split_axis=0, concat_axis=0, tiled=True)]
    ppermute x0 -> x3, waiting for transfers between devices: none -> 9.24 us  [the longest x1 9.14 us: on_device(): from_cross = lax.ppermute(to_cross, 'vis', TO_CROSS)]
    ppermute x0 -> x3, starting transfers between devices: none -> 5.13 us  [the longest x1 5.12 us: on_device(): from_cross = lax.ppermute(to_cross, 'vis', TO_CROSS)]
    unnamed x7 -> x34, local copies, waits for them, and re-layouts: 2.75 us -> 6.76 us
  transfers between devices with their start and end apart: 4 -> 7, of which waited for: 3 -> 5; matrix products, arithmetic and copies ran while one was open for 1% -> 1% of each run, Pallas kernels for 0% -> 11%
where the time goes in v1:
time: 89.6 us; the launch traced here: 89.1 us
  Pallas kernels  32.9 us (37%)
  waiting for transfers between devices  28.9 us (32%)
  starting transfers between devices  18.6 us (21%)
  local copies, waits for them, and re-layouts  6.76 us (8%)
  other arithmetic  1.12 us (1%)
    ppermute x1, waiting for transfers between devices, on_device(): far = lax.ppermute(k0 + r0, 'vis', TO_CHIP)  11.8 us
    all_to_all x1, starting transfers between devices, on_device(): lax.all_to_all(blocks, 'facet', split_axis=0, concat_axis=0, tiled=True)  10.6 us
    pallas_call x1, Pallas kernels, order_rows(): pl.pallas_call(order_kernel, in_specs=[smem] * 3, out_specs=[smem] * 3, o...  9.52 us
    ppermute x1, waiting for transfers between devices, on_device(): from_cross = lax.ppermute(to_cross, 'vis', TO_CROSS)  9.14 us
    pallas_call x2, Pallas kernels, degrid(): pl.pallas_call(functools.partial(degrid_kernel, part=part), in_specs=[sme...  8.85 us
    unnamed x34, local copies, waits for them, and re-layouts  6.76 us
    all_to_all x1, waiting for transfers between devices, on_device(): lax.all_to_all(blocks, 'facet', split_axis=0, concat_axis=0, tiled=True)  6.12 us
    pallas_call x1, Pallas kernels, x_sum(): pl.pallas_call(x_kernel, grid=(NY,), in_specs=[pl.BlockSpec((2, XROWS, YB...  5.39 us
  transfers between devices with their start and end apart: 7, of which 5 were waited for; matrix products, arithmetic and copies ran while one was open for 1% of the time, Pallas kernels for 11%

profile of v1, /device:TPU:1, one launch (start us, length us, event | category | flops | bytes accessed | tf_op | source)
XLA Modules:
  0.0 89.1 jit_solution(13797002914700143163)
XLA Ops:
  0.0 5.4 %x_sum.1 = (f32[128,1024]{1,0:T(8,128)}, f32[128,1024]{1,0:T(8,128)}, f32[128,1024]{1,0:T(8,128)}, f32[128,1024]{1,0:T(8,128)}) custom-call(f32[2,256,1024]{2,1,0:T(8,128)} %facet_ref.1, bf16[4,256,256]{2,1,0:T(8,128)(2,1)} %constant.14.clone.xtab_ref, f32[128,8,256]{2,1,0:T(8,128)} %constant.15.clone.xrot_ref), custom_call_target="tpu_custom_call" | custom-call | tf_op jit(solution)/shard_map/x_sum/pallas_call | solution.py:129
  5.4 1.4 %collective-permute-start.1 = (f32[128,1024]{1,0:T(8,128)}, f32[128,1024]{1,0:T(8,128)S(1)}, u32[]{:S(2)}, u32[]{:S(2)}) collective-permute-start(f32[128,1024]{1,0:T(8,128)} %get-tuple-element.22), channel_id=1, source_target_pairs={{0,1},{1,0},{2,3},{3,2},{4,5},{5,4},{6,7},{7,6},{8,9},{9,8},{10,11... | collective-permute-start | bytes 1572872 | tf_op jit(solution)/shard_map/ppermute | solution.py:398
  6.8 0.1 collective-permute-start
  6.9 1.7 %collective-permute-done.1 = f32[128,1024]{1,0:T(8,128)S(1)} collective-permute-done((f32[128,1024]{1,0:T(8,128)}, f32[128,1024]{1,0:T(8,128)S(1)}, u32[]{:S(2)}, u32[]{:S(2)}) %collective-permute-start.1) | collective-permute-done | bytes 524320 | tf_op jit(solution)/shard_map/ppermute | solution.py:398
  8.6 1.1 %add.3 = f32[128,1024]{1,0:T(8,128)S(1)} add(f32[128,1024]{1,0:T(8,128)} %get-tuple-element.21, f32[128,1024]{1,0:T(8,128)S(1)} %collective-permute-done.1) | non-fusion elementwise | flops 131072 | bytes 1572864 | tf_op jit(solution)/shard_map/add | solution.py:400
  9.7 1.4 %collective-permute-start.2 = (f32[128,1024]{1,0:T(8,128)S(1)}, f32[128,1024]{1,0:T(8,128)S(1)}, u32[]{:S(2)}, u32[]{:S(2)}) collective-permute-start(f32[128,1024]{1,0:T(8,128)S(1)} %add.3), channel_id=1, source_target_pairs={{0,2},{2,0},{1,3},{3,1},{4,6},{6,4},{5,7},{7,5},{8,10},{10,8},{9,1... | collective-permute-start | bytes 1572872 | tf_op jit(solution)/shard_map/ppermute | solution.py:400
  11.1 0.0 collective-permute-done.near_ref
  11.1 11.8 %collective-permute-done.2.far_ref = f32[128,1024]{1,0:T(8,128)S(1)} collective-permute-done((f32[128,1024]{1,0:T(8,128)S(1)}, f32[128,1024]{1,0:T(8,128)S(1)}, u32[]{:S(2)}, u32[]{:S(2)}) %collective-permute-start.2) | collective-permute-done | bytes 524320 | tf_op jit(solution)/shard_map/ppermute | solution.py:400
  22.9 2.2 %copy-done = bf16[16,2,256,256]{3,2,1,0:T(8,128)(2,1)S(1)} copy-done((bf16[16,2,256,256]{3,2,1,0:T(8,128)(2,1)S(1)}, bf16[16,2,256,256]{3,2,1,0:T(8,128)(2,1)}, u32[]{:S(2)}) %copy-start) | copy-done | bytes 4194328
  25.1 1.0 %copy-done.1 = f32[128,1024]{1,0:T(8,128)S(1)} copy-done((f32[128,1024]{1,0:T(8,128)S(1)}, f32[128,1024]{1,0:T(8,128)}, u32[]{:S(2)}) %copy-start.1) | copy-done | bytes 524312
  26.1 0.0 copy-start.8
  26.1 0.0 copy-start.9
  26.2 0.0 copy-start.10
  26.2 5.2 %y_sum.1 = f32[32,64,128]{2,1,0:T(8,128)} custom-call(f32[128,1024]{1,0:T(8,128)S(1)} %copy-done.1, f32[128,1024]{1,0:T(8,128)S(1)} %collective-permute-done.near_ref, f32[128,1024]{1,0:T(8,128)S(1)} %collective-permute-done.2.far_ref, bf16[16,2,256,256]{3,2,1,0:T(8,128)(2,1)S(1)} %copy-done, f32[8,2048]{1,0:T(8,128)S(1)} %copy-done.5), custom_call_target="tpu_custom_call" | custom-call | tf_op jit(solution)/shard_map/y_sum/pallas_call | solution.py:178
  31.4 10.6 %all-to-all-start = ((f32[32,64,128]{2,1,0:T(8,128)}), f32[32,64,128]{2,1,0:T(8,128)S(1)}, u32[]{:S(2)}, u32[]{:S(2)}) async-start(f32[32,64,128]{2,1,0:T(8,128)} %y_sum.1), calls=%async_computation | async-start | bytes 2097152 | tf_op jit(solution)/shard_map/all_to_all | solution.py:403
  42.7 9.5 %order_rows.1 = (s32[600]{0:T(1024)}, s32[600]{0:T(1024)}, s32[2]{0:T(128)}) custom-call(s32[1,1]{1,0:T(1,128)S(6)} %copy.15.counts_ref, s32[1,1,512]{2,1,0:T(1,128)} %wplanes_ref.5, s32[1,1,512]{2,1,0:T(1,128)} %bitcast.3), custom_call_target="tpu_custom_call" | custom-call | flops 20000000 | bytes 20000000 | tf_op jit(solution)/shard_map/order_rows/pallas_call | solution.py:254
  52.2 6.1 %all-to-all-done.blocks_ref = f32[32,64,128]{2,1,0:T(8,128)S(1)} async-done(((f32[32,64,128]{2,1,0:T(8,128)}), f32[32,64,128]{2,1,0:T(8,128)S(1)}, u32[]{:S(2)}, u32[]{:S(2)}) %all-to-all-start) | async-done | bytes 1048608 | tf_op jit(solution)/shard_map/all_to_all | solution.py:403
  58.3 1.8 %make_planes.1.planes_ref = bf16[8,128,256]{2,1,0:T(8,128)(2,1)S(1)} custom-call(s32[4,8]{1,0:T(4,128)S(1)} %bitcast.2, f32[32,64,128]{2,1,0:T(8,128)S(1)} %all-to-all-done.blocks_ref, f32[2,64,512]{2,1,0:T(8,128)S(1)} %copy-done.2, f32[128,128]{1,0:T(8,128)S(1)} %copy-done.6, f32[128,256]{1,0:T(8,128)S(1)} %copy-done.4), custom_call_target="tpu_custom_call" | custom-call | tf_op jit(solution)/shard_map/make_planes/pallas_call | solution.py:291
  60.2 0.7 copy-done.11
  60.8 0.7 copy-done.12
  61.5 0.6 copy-done.13
  62.1 3.2 %degrid_far.1 = (f32[256,256]{1,0:T(8,128)S(1)}, f32[256,256]{1,0:T(8,128)S(1)}) custom-call(s32[600]{0:T(1024)S(1)} %copy-done.11, s32[600]{0:T(1024)S(1)} %copy-done.12, s32[2]{0:T(128)S(1)} %copy-done.13, s32[1,1,512]{2,1,0:T(1,128)S(1)} %copy-done.10, bf16[8,128,256]{2,1,0:T(8,128)(2,1)S(1)} %make_planes.1.planes_ref, ...), custom_call_target="tpu_custom_call" | custom-call | flops 4000000000 | bytes 2000000 | tf_op jit(solution)/shard_map/degrid_far/pallas_call | solution.py:355
  65.3 5.7 %degrid_near.1 = (f32[256,256]{1,0:T(8,128)S(1)}, f32[256,256]{1,0:T(8,128)S(1)}) custom-call(s32[600]{0:T(1024)S(1)} %copy-done.11, s32[600]{0:T(1024)S(1)} %copy-done.12, s32[2]{0:T(128)S(1)} %copy-done.13, s32[1,1,512]{2,1,0:T(1,128)S(1)} %copy-done.10, bf16[8,128,256]{2,1,0:T(8,128)(2,1)S(1)} %make_planes.1.planes_ref, ...), custom_call_target="tpu_custom_call" | custom-call | flops 4000000000 | bytes 2000000 | tf_op jit(solution)/shard_map/degrid_near/pallas_call | solution.py:355
  71.0 0.7 copy-done.3
  71.7 0.0 collective-permute-start.4
  71.7 5.1 %collective-permute-start.5 = (f32[256,256]{1,0:T(8,128)S(1)}, f32[256,256]{1,0:T(8,128)S(1)}, u32[]{:S(2)}, u32[]{:S(2)}) collective-permute-start(f32[256,256]{1,0:T(8,128)S(1)} %get-tuple-element.26), channel_id=1, source_target_pairs={{0,3},{3,0},{1,2},{2,1},{4,7},{7,4},{5,6},{6,5},{8,11},{11,8},{9,1... | collective-permute-start | bytes 786440 | tf_op jit(solution)/shard_map/ppermute | solution.py:407
  76.8 0.0 collective-permute-start.3
  76.9 0.1 collective-permute-done.4.chip_ref
  76.9 9.1 %collective-permute-done.5.cross_ref = f32[256,256]{1,0:T(8,128)S(1)} collective-permute-done((f32[256,256]{1,0:T(8,128)S(1)}, f32[256,256]{1,0:T(8,128)S(1)}, u32[]{:S(2)}, u32[]{:S(2)}) %collective-permute-start.5) | collective-permute-done | bytes 262176 | tf_op jit(solution)/shard_map/ppermute | solution.py:407
  86.1 0.7 copy-done.15
  86.8 0.1 copy-done.16
  86.9 2.2 %gather_rows.1 = f32[1,1,4,256,256]{4,3,2,1,0:T(8,128)} custom-call(f32[256,256]{1,0:T(8,128)} %copy-done.3, f32[256,256]{1,0:T(8,128)} %copy-done.16, f32[256,256]{1,0:T(8,128)} %copy-done.14, f32[256,256]{1,0:T(8,128)} %copy-done.15), custom_call_target="tpu_custom_call" | custom-call | tf_op jit(solution)/shard_map/gather_rows/pallas_call | solution.py:380
  (24 shorter events, 0.0 us)
Async XLA Ops:
  0.0 22.9 %copy-start.5 = (f32[8,2048]{1,0:T(8,128)S(1)}, f32[8,2048]{1,0:T(8,128)}, u32[]{:S(2)}) copy-start(f32[8,2048]{1,0:T(8,128)} %constant.17.clone.yrot_ref) | copy-start | bytes 196612
  5.4 3.2 %collective-permute-start.1 = (f32[128,1024]{1,0:T(8,128)}, f32[128,1024]{1,0:T(8,128)S(1)}, u32[]{:S(2)}, u32[]{:S(2)}) collective-permute-start(f32[128,1024]{1,0:T(8,128)} %get-tuple-element.22), channel_id=1, source_target_pairs={{0,1},{1,0},{2,3},{3,2},{4,5},{5,4},{6,7},{7,6},{8,9},{9,8},{10,11... | collective-permute-start | bytes 1572872 | tf_op jit(solution)/shard_map/ppermute | solution.py:398
  6.8 4.3 %collective-permute-start = (f32[128,1024]{1,0:T(8,128)}, f32[128,1024]{1,0:T(8,128)S(1)}, u32[]{:S(2)}, u32[]{:S(2)}) collective-permute-start(f32[128,1024]{1,0:T(8,128)} %get-tuple-element.20), channel_id=1, source_target_pairs={{0,1},{1,0},{2,3},{3,2},{4,5},{5,4},{6,7},{7,6},{8,9},{9,8},{10,11... | collective-permute-start | bytes 1572872 | tf_op jit(solution)/shard_map/ppermute | solution.py:399
  9.7 13.2 %collective-permute-start.2 = (f32[128,1024]{1,0:T(8,128)S(1)}, f32[128,1024]{1,0:T(8,128)S(1)}, u32[]{:S(2)}, u32[]{:S(2)}) collective-permute-start(f32[128,1024]{1,0:T(8,128)S(1)} %add.3), channel_id=1, source_target_pairs={{0,2},{2,0},{1,3},{3,1},{4,6},{6,4},{5,7},{7,5},{8,10},{10,8},{9,1... | collective-permute-start | bytes 1572872 | tf_op jit(solution)/shard_map/ppermute | solution.py:400
  22.9 2.2 %copy-start = (bf16[16,2,256,256]{3,2,1,0:T(8,128)(2,1)S(1)}, bf16[16,2,256,256]{3,2,1,0:T(8,128)(2,1)}, u32[]{:S(2)}) copy-start(bf16[16,2,256,256]{3,2,1,0:T(8,128)(2,1)} %constant.16.clone.ytab_ref) | copy-start | bytes 12582916
  25.1 1.0 %copy-start.1 = (f32[128,1024]{1,0:T(8,128)S(1)}, f32[128,1024]{1,0:T(8,128)}, u32[]{:S(2)}) copy-start(f32[128,1024]{1,0:T(8,128)} %get-tuple-element.19.kept_ref) | copy-start | bytes 1572868
  26.1 32.2 %copy-start.2 = (f32[2,64,512]{2,1,0:T(8,128)S(1)}, f32[2,64,512]{2,1,0:T(8,128)}, u32[]{:S(2)}) copy-start(f32[2,64,512]{2,1,0:T(8,128)} %constant.18.clone.screens_ref) | copy-start | bytes 786436
  26.1 32.2 %copy-start.4 = (f32[128,256]{1,0:T(8,128)S(1)}, f32[128,256]{1,0:T(8,128)}, u32[]{:S(2)}) copy-start(f32[128,256]{1,0:T(8,128)} %constant.20.clone.right_ref) | copy-start | bytes 393220
  26.1 32.2 %copy-start.6 = (f32[128,128]{1,0:T(8,128)S(1)}, f32[128,128]{1,0:T(8,128)}, u32[]{:S(2)}) copy-start(f32[128,128]{1,0:T(8,128)} %constant.19.clone.left_ref) | copy-start | bytes 196612
  26.1 32.2 %copy-start.7 = (s32[4,1,8]{2,1,0:T(1,128)S(1)}, s32[4,1,8]{2,1,0:T(1,128)}, u32[]{:S(2)}) copy-start(s32[4,1,8]{2,1,0:T(1,128)} %param.15) | copy-start | bytes 388
  26.1 34.0 %copy-start.8 = (s32[2,1,1,512,128]{4,3,2,1,0:T(8,128)S(1)}, s32[2,1,1,512,128]{4,3,2,1,0:T(8,128)}, u32[]{:S(2)}) copy-start(s32[2,1,1,512,128]{4,3,2,1,0:T(8,128)} %offsets_ref.3) | copy-start | bytes 1572868
  26.1 34.0 %copy-start.9 = (f32[2,1,1,512,128]{4,3,2,1,0:T(8,128)S(1)}, f32[2,1,1,512,128]{4,3,2,1,0:T(8,128)}, u32[]{:S(2)}) copy-start(f32[2,1,1,512,128]{4,3,2,1,0:T(8,128)} %frac_ref.3) | copy-start | bytes 1572868
  26.2 34.0 %copy-start.10 = (s32[1,1,512]{2,1,0:T(1,128)S(1)}, s32[1,1,512]{2,1,0:T(1,128)}, u32[]{:S(2)}) copy-start(s32[1,1,512]{2,1,0:T(1,128)} %wplanes_ref.5) | copy-start | bytes 6148
  31.4 26.9 %all-to-all-start = ((f32[32,64,128]{2,1,0:T(8,128)}), f32[32,64,128]{2,1,0:T(8,128)S(1)}, u32[]{:S(2)}, u32[]{:S(2)}) async-start(f32[32,64,128]{2,1,0:T(8,128)} %y_sum.1), calls=%async_computation | async-start | bytes 2097152 | tf_op jit(solution)/shard_map/all_to_all | solution.py:403
  60.1 0.7 copy-start.11
  60.8 0.7 copy-start.12
  61.5 0.6 copy-start.13
  71.0 0.7 copy-start.3
  71.7 5.2 %collective-permute-start.4 = (f32[256,256]{1,0:T(8,128)S(1)}, f32[256,256]{1,0:T(8,128)S(1)}, u32[]{:S(2)}, u32[]{:S(2)}) collective-permute-start(f32[256,256]{1,0:T(8,128)S(1)} %get-tuple-element.25), channel_id=1, source_target_pairs={{0,2},{2,0},{1,3},{3,1},{4,6},{6,4},{5,7},{7,5},{8,10},{10,8},{9,1... | collective-permute-start | bytes 786440 | tf_op jit(solution)/shard_map/ppermute | solution.py:406
  71.7 14.4 %collective-permute-start.5 = (f32[256,256]{1,0:T(8,128)S(1)}, f32[256,256]{1,0:T(8,128)S(1)}, u32[]{:S(2)}, u32[]{:S(2)}) collective-permute-start(f32[256,256]{1,0:T(8,128)S(1)} %get-tuple-element.26), channel_id=1, source_target_pairs={{0,3},{3,0},{1,2},{2,1},{4,7},{7,4},{5,6},{6,5},{8,11},{11,8},{9,1... | collective-permute-start | bytes 786440 | tf_op jit(solution)/shard_map/ppermute | solution.py:407
  76.8 9.2 %collective-permute-start.3 = (f32[256,256]{1,0:T(8,128)S(1)}, f32[256,256]{1,0:T(8,128)S(1)}, u32[]{:S(2)}, u32[]{:S(2)}) collective-permute-start(f32[256,256]{1,0:T(8,128)S(1)} %get-tuple-element.24), channel_id=1, source_target_pairs={{0,1},{1,0},{2,3},{3,2},{4,5},{5,4},{6,7},{7,6},{8,9},{9,8},{10,11... | collective-permute-start | bytes 786440 | tf_op jit(solution)/shard_map/ppermute | solution.py:409
  76.9 9.2 %copy-start.14 = (f32[256,256]{1,0:T(8,128)}, f32[256,256]{1,0:T(8,128)S(1)}, u32[]{:S(2)}) copy-start(f32[256,256]{1,0:T(8,128)S(1)} %collective-permute-done.4.chip_ref) | copy-start | bytes 786436
  86.1 0.7 copy-start.15
  86.1 0.8 copy-start.16

commit v2 on v1

--- a/solution.py
+++ b/solution.py
@@ -98,119 +98,143 @@
     return jnp.dot(a, b, preferred_element_type=F32)
 
 
-def x_kernel(facet_ref, xtab_ref, xrot_ref, s0_ref, s1_ref, k0_ref, k1_ref, rot_ref):
+def x_kernel(facet_ref, xtab_ref, xrot_ref, send_ref, k0_ref, k1_ref, rhs_ref, tab_ref, turn_ref, rot_ref, sems, *, half):
     vis = lax.axis_index("vis")
     x_lo, core = vis // 2, vis % 2
+    loads = [
+        pltpu.make_async_copy(xtab_ref, tab_ref, sems.at[0]),
+        pltpu.make_async_copy(xrot_ref.at[lax.axis_index("facet") * N_VIS + vis], turn_ref, sems.at[1]),
+    ]
+    for i in range(2):
+        columns = pl.ds((2 * half + i) * YBLK, YBLK)
+        loads.append(pltpu.make_async_copy(facet_ref.at[:, :, columns], rhs_ref.at[i], sems.at[2 + i]))
+    for load in loads:
+        load.start()
+    loads[1].wait()
+    rot_ref[...] = turn_ref[...].T
+    loads[0].wait()
+    order = row_order(x_lo, core)
+    full = jnp.concatenate([tab_ref[r] for r in order], 0)
+    high = jnp.concatenate([tab_ref[r, : 2 * SUB] for r in order], 0)
+    outs = (send_ref.at[: 2 * SUB], send_ref.at[2 * SUB :], k0_ref, k1_ref)
+    for block in range(2):
+        loads[2 + block].wait()
+        a = []
+        for part in range(2):
+            hi, lo = split(rhs_ref[block, part])
+            both = dot(full, hi).reshape(N_VIS, 2, 2 * SUB, YBLK)
+            a.append(both[:, 0] + both[:, 1] + dot(high, lo).reshape(N_VIS, 2 * SUB, YBLK))
+        for i, out in enumerate(outs):
+            re = a[0][i, :SUB] + a[1][i, SUB:]
+            im = a[1][i, :SUB] - a[0][i, SUB:]
+            cosine = rot_ref[i * SUB : (i + 1) * SUB, 0:1]
+            sine = rot_ref[i * SUB : (i + 1) * SUB, 1:2]
+            out[:SUB, block * YBLK : (block + 1) * YBLK] = re * cosine + im * sine
+            out[SUB:, block * YBLK : (block + 1) * YBLK] = im * cosine - re * sine
+
+
+def x_sum(half, facet_image, xtab, xrot):
+    vmem = pl.BlockSpec(memory_space=pltpu.VMEM)
+    kept = jax.ShapeDtypeStruct((2 * SUB, FP // 2), F32)
+    return pl.pallas_call(
+        functools.partial(x_kernel, half=half),
+        in_specs=[pl.BlockSpec(memory_space=pltpu.HBM)] * 3,
+        out_specs=[vmem] * 3,
+        out_shape=[jax.ShapeDtypeStruct((4 * SUB, FP // 2), F32), kept, kept],
+        scratch_shapes=[
+            pltpu.VMEM((2, 2, XROWS, YBLK), F32),
+            pltpu.VMEM(xtab.shape, BF16),
+            pltpu.VMEM(xrot.shape[1:], F32),
+            pltpu.VMEM((N_VIS * SUB, 8), F32),
+            pltpu.SemaphoreType.DMA((4,)),
+        ],
+        compiler_params=pltpu.CompilerParams(vmem_limit_bytes=(60, 20)[half] * 1024 * 1024),
+        cost_estimate=pl.CostEstimate(flops=2_000_000_000, bytes_accessed=2_000_000, transcendentals=0),
+        name="x_sum_" + "ab"[half],
+    )(facet_image, xtab, xrot)
+
+
+PAIRS = 4
+
+
+def y_kernel(*refs, half):
+    if half == 0:
+        kept_ref, near_ref, far_ref, ytab_ref, yrot_ref, out_ref, lhs_ref = refs
+    else:
+        kept_ref, near_ref, far_ref, ytab_ref, yrot_ref, first_ref, out_ref, lhs_ref = refs
 
     @pl.when(pl.program_id(0) == 0)
     def _():
-        rot_ref[...] = xrot_ref[lax.axis_index("facet") * N_VIS + vis].T
-
-    rhs = [split(facet_ref[0]), split(facet_ref[1])]
-    order = row_order(x_lo, core)
-    full = jnp.concatenate([xtab_ref[r] for r in order], 0)
-    high = jnp.concatenate([xtab_ref[r, : 2 * SUB] for r in order], 0)
-    a = []
-    for hi, lo in rhs:
-        both = dot(full, hi).reshape(N_VIS, 2, 2 * SUB, YBLK)
-        a.append(both[:, 0] + both[:, 1] + dot(high, lo).reshape(N_VIS, 2 * SUB, YBLK))
-    for i, out in enumerate((s0_ref, s1_ref, k0_ref, k1_ref)):
-        re = a[0][i, :SUB] + a[1][i, SUB:]
-        im = a[1][i, :SUB] - a[0][i, SUB:]
-        cosine = rot_ref[i * SUB : (i + 1) * SUB, 0:1]
-        sine = rot_ref[i * SUB : (i + 1) * SUB, 1:2]
-        out[:SUB] = re * cosine + im * sine
-        out[SUB:] = im * cosine - re * sine
-
-
-def x_sum(facet_image, xtab, xrot):
-    out = jax.ShapeDtypeStruct((2 * SUB, FP), F32)
-    block = pl.BlockSpec((2 * SUB, YBLK), lambda i: (0, i))
-    return pl.pallas_call(
-        x_kernel,
-        grid=(NY,),
-        in_specs=[
-            pl.BlockSpec((2, XROWS, YBLK), lambda i: (0, 0, i)),
-            pl.BlockSpec(xtab.shape, lambda i: (0, 0, 0)),
-            pl.BlockSpec(xrot.shape, lambda i: (0, 0, 0)),
-        ],
-        out_specs=[block] * 4,
-        out_shape=[out] * 4,
-        scratch_shapes=[pltpu.VMEM((N_VIS * SUB, 8), F32)],
-        compiler_params=pltpu.CompilerParams(vmem_limit_bytes=60 * 1024 * 1024),
-        name="x_sum",
-    )(facet_image, xtab, xrot)
-
-
-def y_kernel(kept_ref, near_ref, far_ref, ytab_ref, yrot_ref, out_ref, lhs_ref):
-    @pl.when(pl.program_id(0) == 0)
-    def _():
-        total = kept_ref[...] + near_ref[...] + far_ref[...]
-        hi, lo = split(total)
-        for y in range(NY):
-            lhs_ref[y * 128 : (y + 1) * 128] = hi[:, y * YBLK : (y + 1) * YBLK]
-            lhs_ref[NY * 128 + y * 128 : NY * 128 + (y + 1) * 128] = lo[:, y * YBLK : (y + 1) * YBLK]
-
-    half = NY * 128
-    first = lax.broadcasted_iota(jnp.int32, (64, 128), 1) < 64
-    lhs = jnp.concatenate([lhs_ref[:half], lhs_ref[half:], lhs_ref[:half]], 1)
+        hi, lo = split(kept_ref[...] + near_ref[...] + far_ref[...])
+        for y in range(2):
+            now = slice(y * YBLK, (y + 1) * YBLK)
+            lhs_ref[y * 128 : (y + 1) * 128] = jnp.concatenate([hi[:, now], lo[:, now], hi[:, now]], 1)
+
+    left_half = lax.broadcasted_iota(jnp.int32, (64, 128), 1) < 64
     for w in range(PAIRS):
-        part = dot(lhs, jnp.concatenate([ytab_ref[w, 0], ytab_ref[w, 0], ytab_ref[w, 1]], 0))
-        re = part[0:64, :128] + part[64:128, 128:]
-        im = part[64:128, :128] - part[0:64, 128:]
-        for y in range(1, NY):
+        part = dot(lhs_ref[...], jnp.concatenate([ytab_ref[w, 0], ytab_ref[w, 0], ytab_ref[w, 1]], 0))
+        re = im = None
+        for y in range(2):
             now = part[y * 128 : (y + 1) * 128]
             gre = now[0:64, :128] + now[64:128, 128:]
             gim = now[64:128, :128] - now[0:64, 128:]
-            cosine = yrot_ref[y : y + 1, w * 128 : (w + 1) * 128]
-            sine = yrot_ref[4 + y : 5 + y, w * 128 : (w + 1) * 128]
-            re = re + gre * cosine + gim * sine
-            im = im + gim * cosine - gre * sine
-        out_ref[2 * w] = jnp.where(first, re, pltpu.roll(im, 64, 1))
-        out_ref[2 * w + 1] = jnp.where(first, pltpu.roll(re, 64, 1), im)
-
-
-PAIRS = 4
-
-
-def y_sum(kept, near, far, ytab, yrot):
-    whole = pl.BlockSpec((2 * SUB, FP), lambda i: (0, 0))
-    return pl.pallas_call(
-        y_kernel,
+            quarter = 2 * half + y
+            if quarter == 0:
+                re, im = gre, gim
+                continue
+            cosine = yrot_ref[quarter : quarter + 1, w * 128 : (w + 1) * 128]
+            sine = yrot_ref[4 + quarter : 5 + quarter, w * 128 : (w + 1) * 128]
+            turned_re, turned_im = gre * cosine + gim * sine, gim * cosine - gre * sine
+            re, im = (turned_re, turned_im) if re is None else (re + turned_re, im + turned_im)
+        even = jnp.where(left_half, re, pltpu.roll(im, 64, 1))
+        odd = jnp.where(left_half, pltpu.roll(re, 64, 1), im)
+        if half == 1:
+            even, odd = even + first_ref[2 * w], odd + first_ref[2 * w + 1]
+        out_ref[2 * w] = even
+        out_ref[2 * w + 1] = odd
+
+
+def y_sum(half, kept, received, far, ytab, yrot, *first):
+    whole = pl.BlockSpec((2 * SUB, FP // 2), lambda i: (0, 0))
+    columns = pl.BlockSpec((2 * PAIRS, SUB, 2 * SUB), lambda i: (i, 0, 0))
+    return pl.pallas_call(
+        functools.partial(y_kernel, half=half),
         grid=(NCOL // 2 // PAIRS,),
         in_specs=[
             whole,
-            whole,
+            pl.BlockSpec((2 * SUB, FP // 2), lambda i: (1, 0)),
             whole,
             pl.BlockSpec((PAIRS, 2, YBLK, 256), lambda i: (i, 0, 0, 0)),
             pl.BlockSpec((8, 128 * PAIRS), lambda i: (0, i)),
-        ],
-        out_specs=pl.BlockSpec((2 * PAIRS, SUB, 2 * SUB), lambda i: (i, 0, 0)),
+        ]
+        + [columns] * len(first),
+        out_specs=columns,
         out_shape=jax.ShapeDtypeStruct((NCOL, SUB, 2 * SUB), F32),
-        scratch_shapes=[pltpu.VMEM((2 * NY * 128, YBLK), BF16)],
+        scratch_shapes=[pltpu.VMEM((2 * 128, 3 * YBLK), BF16)],
         compiler_params=pltpu.CompilerParams(vmem_limit_bytes=VMEM_LIMIT),
-        name="y_sum",
-    )(kept, near, far, ytab, yrot)
+        cost_estimate=pl.CostEstimate(flops=3_000_000_000, bytes_accessed=6_000_000, transcendentals=0),
+        name="y_sum_" + "ab"[half],
+    )(kept, received, far, ytab, yrot, *first)
 
 
 TAPER = math.sqrt(0.5 * math.log2(math.e)) / 1.6
 STEP = 32
-SPAN = ROWS + 2 * NW + 2 * STEP
-JUNK = 2 * 2 * CAP
-
-
-def order_kernel(counts_ref, wplanes_ref, owners_ref, row_ref, place_ref, ends_ref, key_ref, fill_ref):
+SPAN = ROWS + N_VIS * (NW + STEP)
+ENDS = SPAN + 8
+JUNK = 2 * CAP
+
+
+def order_kernel(counts_ref, wplanes_ref, owners_ref, order_ref, key_ref, fill_ref):
     vis = lax.axis_index("vis")
     count = counts_ref[0, 0]
-    for i in range(2 * NW):
+    for i in range(N_VIS * NW):
         key_ref[i] = 0
     for i in range(N_VIS):
         fill_ref[i] = 0
 
     def clear(i, carry):
         for j in range(8):
-            row_ref[i * 8 + j] = 0
-            place_ref[i * 8 + j] = JUNK
+            order_ref[i * 8 + j] = JUNK * ROWS
         return carry
 
     lax.fori_loop(0, SPAN // 8, clear, 0)
@@ -218,19 +242,20 @@
     def tally(i, carry):
         for j in range(8):
             n = i * 8 + j
-            key = wplanes_ref[0, 0, n] + NW * (1 - ((owners_ref[0, 0, n] ^ vis) >> 1))
+            key = wplanes_ref[0, 0, n] + NW * (3 - (owners_ref[0, 0, n] ^ vis))
             key_ref[key] = key_ref[key] + jnp.where(n < count, 1, 0)
         return carry
 
     lax.fori_loop(0, ROWS // 8, tally, 0)
     start = jnp.int32(0)
-    for part in range(2):
+    order_ref[ENDS] = 0
+    for part in range(N_VIS):
         for w in range(NW):
             held = key_ref[part * NW + w]
             key_ref[part * NW + w] = start
             start = start + ((held + 1) & ~1)
         start = (start + STEP - 1) & ~(STEP - 1)
-        ends_ref[part] = start // STEP
+        order_ref[ENDS + 1 + part] = start // STEP
 
     def deal(i, carry):
         for j in range(8):
@@ -238,11 +263,10 @@
             apart = owners_ref[0, 0, n] ^ vis
             slot = fill_ref[apart]
             fill_ref[apart] = slot + 1
-            key = wplanes_ref[0, 0, n] + NW * (1 - (apart >> 1))
+            key = wplanes_ref[0, 0, n] + NW * (3 - apart)
             at = jnp.where(n < count, key_ref[key], SPAN)
             key_ref[key] = key_ref[key] + jnp.where(n < count, 1, 0)
-            row_ref[at] = n
-            place_ref[at] = (apart & 1) * (2 * CAP) + slot + (slot & ~7)
+            order_ref[at] = (slot + (slot & ~7)) * ROWS + n
         return carry
 
     lax.fori_loop(0, ROWS // 8, deal, 0)
@@ -250,14 +274,14 @@
 
 def order_rows(counts, wplanes, owners):
     smem = pl.BlockSpec(memory_space=pltpu.SMEM)
-    flat = jax.ShapeDtypeStruct((SPAN + 8,), jnp.int32)
     return pl.pallas_call(
         order_kernel,
         in_specs=[smem] * 3,
-        out_specs=[smem] * 3,
-        out_shape=[flat, flat, jax.ShapeDtypeStruct((2,), jnp.int32)],
-        scratch_shapes=[pltpu.SMEM((2 * NW,), jnp.int32), pltpu.SMEM((N_VIS,), jnp.int32)],
+        out_specs=smem,
+        out_shape=jax.ShapeDtypeStruct((ENDS + 8,), jnp.int32),
+        scratch_shapes=[pltpu.SMEM((N_VIS * NW,), jnp.int32), pltpu.SMEM((N_VIS,), jnp.int32)],
         cost_estimate=pl.CostEstimate(flops=20_000_000, bytes_accessed=20_000_000, transcendentals=0),
+        compiler_params=pltpu.CompilerParams(vmem_limit_bytes=8 * 1024 * 1024),
         name="order_rows",
     )(counts, wplanes, owners)
 
@@ -299,7 +323,7 @@
 
 
 def degrid_kernel(
-    row_ref, place_ref, ends_ref, wplanes_ref, planes_ref, offsets_ref, frac_ref, out0_ref, out1_ref, rows_ref, *, part
+    order_ref, wplanes_ref, planes_ref, offsets_ref, frac_ref, out_ref, rows_ref, *, part
 ):
     rows_ref[...] = jnp.zeros_like(rows_ref)
     cell = lax.broadcasted_iota(jnp.int32, (8, CH), 0)
@@ -315,7 +339,8 @@
     def body(group, carry):
         base = group * STEP
         for i in range(0, STEP, 2):
-            pair = [row_ref[base + i], row_ref[base + i + 1]]
+            packed = [order_ref[base + i], order_ref[base + i + 1]]
+            pair = [word & (ROWS - 1) for word in packed]
             sides, high, low = [], [], []
             for n in pair:
                 uval, ublock = taps(0, n)
@@ -335,33 +360,31 @@
                     here = vblock == j
                     are = jnp.where(here, t[8 * j : 8 * j + 8], are)
                     aim = jnp.where(here, t[64 + 8 * j : 72 + 8 * j], aim)
-                place = place_ref[base + i + side]
+                place = packed[side] >> 9
                 rows_ref[pl.ds(place, 1), :] = jnp.sum(are * vval, 0, keepdims=True)
                 rows_ref[pl.ds(place + 8, 1), :] = jnp.sum(aim * vval, 0, keepdims=True)
         return carry
 
-    lax.fori_loop(0 if part == 0 else ends_ref[0], ends_ref[part], body, 0)
-
-    for side, out in enumerate((out0_ref, out1_ref)):
-        tiles = rows_ref[side * 2 * CAP : (side + 1) * 2 * CAP].reshape(CAP // 8, 2, 8, CH)
-        out[:, :CH] = tiles[:, 0].reshape(CAP, CH)
-        out[:, CH:] = tiles[:, 1].reshape(CAP, CH)
-
-
-def degrid(part, row, place, ends, wplanes, planes, offsets, frac):
+    lax.fori_loop(order_ref[ENDS + part], order_ref[ENDS + part + 1], body, 0)
+
+    tiles = rows_ref[: 2 * CAP].reshape(CAP // 8, 2, 8, CH)
+    out_ref[:, :CH] = tiles[:, 0].reshape(CAP, CH)
+    out_ref[:, CH:] = tiles[:, 1].reshape(CAP, CH)
+
+
+def degrid(part, order, wplanes, planes, offsets, frac):
     smem = pl.BlockSpec(memory_space=pltpu.SMEM)
     vmem = pl.BlockSpec(memory_space=pltpu.VMEM)
-    out = jax.ShapeDtypeStruct((CAP, 2 * CH), F32)
     return pl.pallas_call(
         functools.partial(degrid_kernel, part=part),
-        in_specs=[smem] * 4 + [vmem] * 3,
-        out_specs=[vmem] * 2,
-        out_shape=[out] * 2,
-        scratch_shapes=[pltpu.VMEM((2 * 2 * CAP + 16, CH), F32)],
+        in_specs=[smem] * 2 + [vmem] * 3,
+        out_specs=vmem,
+        out_shape=jax.ShapeDtypeStruct((CAP, 2 * CH), F32),
+        scratch_shapes=[pltpu.VMEM((2 * CAP + 16, CH), F32)],
         compiler_params=pltpu.CompilerParams(vmem_limit_bytes=VMEM_LIMIT),
-        cost_estimate=pl.CostEstimate(flops=4_000_000_000, bytes_accessed=2_000_000, transcendentals=0),
-        name="degrid_" + ("far", "near")[part],
-    )(row, place, ends, wplanes, planes, offsets, frac)
+        cost_estimate=pl.CostEstimate(flops=2_500_000_000, bytes_accessed=2_000_000, transcendentals=0),
+        name="degrid_" + ("cross", "chip", "core", "own")[part],
+    )(order, wplanes, planes, offsets, frac)
 
 
 def gather_kernel(self_ref, core_ref, chip_ref, cross_ref, out_ref, sems):
@@ -383,6 +406,7 @@
         out_specs=pl.BlockSpec(memory_space=pl.ANY),
         out_shape=jax.ShapeDtypeStruct((1, 1, N_VIS, CAP, 2 * CH), F32),
         scratch_shapes=[pltpu.SemaphoreType.DMA((N_VIS,))],
+        compiler_params=pltpu.CompilerParams(vmem_limit_bytes=8 * 1024 * 1024),
         name="gather_rows",
     )(*blocks)
 
@@ -394,18 +418,23 @@
 
 def on_device(facet_image, contributions, counts, wplanes, kernel_offsets, kernel_frac, owners):
     xtab, xrot, ytab, yrot, screens, left, right = [jnp.asarray(t) for t in tables()]
-    s0, s1, k0, k1 = x_sum(facet_image, xtab, xrot)
-    r0 = lax.ppermute(s0, "vis", TO_CORE)
-    r1 = lax.ppermute(s1, "vis", TO_CORE)
-    far = lax.ppermute(k0 + r0, "vis", TO_CHIP)
-    blocks = y_sum(k1, r1, far, ytab, yrot)
-    row, place, ends = order_rows(counts, wplanes, owners[..., 0])
+    parts = []
+    for half in range(2):
+        send, k0, k1 = x_sum(half, facet_image, xtab, xrot)
+        received = lax.ppermute(send, "vis", TO_CORE)
+        far = lax.ppermute(k0 + received[: 2 * SUB], "vis", TO_CHIP)
+        parts.append((k1, received, far))
+    blocks = y_sum(0, *parts[0], ytab, yrot)
+    blocks = y_sum(1, *parts[1], ytab, yrot, blocks)
+    order = order_rows(counts, wplanes, owners[..., 0])
     arrived = lax.all_to_all(blocks, "facet", split_axis=0, concat_axis=0, tiled=True)
     planes = make_planes(contributions[:, 0, :], arrived, screens, left, right)
-    to_chip, to_cross = degrid(0, row, place, ends, wplanes, planes, kernel_offsets, kernel_frac)
+    to_cross, to_chip, to_core, own = [
+        degrid(part, order, wplanes, planes, kernel_offsets, kernel_frac) for part in range(N_VIS)
+    ]
+    from_cross = lax.ppermute(to_cross, "vis", TO_CROSS)
     from_chip = lax.ppermute(to_chip, "vis", TO_CHIP)
-    from_cross = lax.ppermute(to_cross, "vis", TO_CROSS)
-    own, to_core = degrid(1, row, place, ends, wplanes, planes, kernel_offsets, kernel_frac)
+    to_core, from_cross = lax.optimization_barrier((to_core, from_cross))
     from_core = lax.ppermute(to_core, "vis", TO_CORE)
     return gather_rows(own, from_core, from_chip, from_cross)
 

time: 89.6 us -> 72.7 us (0.81)
  waiting for transfers between devices: 28.9 us -> 17 us
  local copies, waits for them, and re-layouts: 6.76 us -> 0.07 us
  starting transfers between devices: 18.6 us -> 20.7 us
  other arithmetic: 1.12 us -> 0.07 us
    ppermute x1, waiting for transfers between devices: 9.14 us -> 0.01 us  [on_device(): from_cross = lax.ppermute(to_cross, 'vis', TO_CROSS)]
    unnamed x34 -> x30, local copies, waits for them, and re-layouts: 6.76 us -> 0.07 us
    ppermute x3 -> x4, waiting for transfers between devices: 13.5 us -> 7.49 us  [the longest x2 7.04 us: on_device(): far = lax.ppermute(k0 + received[:2 * SUB], 'vis', TO_CHIP)]
    ppermute x1, starting transfers between devices: 5.12 us -> 1.88 us  [on_device(): from_cross = lax.ppermute(to_cross, 'vis', TO_CROSS)]
    ppermute x1, waiting for transfers between devices: 0.09 us -> 2.32 us  [on_device(): from_chip = lax.ppermute(to_chip, 'vis', TO_CHIP)]
    ppermute x1, starting transfers between devices: 0.01 us -> 2.09 us  [on_device(): from_core = lax.ppermute(to_core, 'vis', TO_CORE)]
    ppermute x1, starting transfers between devices: 0.01 us -> 1.66 us  [on_device(): from_chip = lax.ppermute(to_chip, 'vis', TO_CHIP)]
    ppermute x3 -> x4, starting transfers between devices: 2.87 us -> 4.38 us  [the longest x2 2.76 us: on_device(): far = lax.ppermute(k0 + received[:2 * SUB], 'vis', TO_CHIP)]
  transfers between devices with their start and end apart: 7 -> 8, of which waited for: 5 -> 5; matrix products, arithmetic and copies ran while one was open for 1% -> 0% of each run, Pallas kernels for 11% -> 28%
where the time goes in v2:
time: 72.7 us; the launch traced here: 71.8 us
  Pallas kernels  33.1 us (46%)
  starting transfers between devices  20.7 us (28%)
  waiting for transfers between devices  17 us (23%)
  between operations  0.86 us (1%)
    all_to_all x1, starting transfers between devices, on_device(): lax.all_to_all(blocks, 'facet', split_axis=0, concat_axis=0, tiled=True)  10.7 us
    pallas_call x4, Pallas kernels, degrid(): pl.pallas_call(functools.partial(degrid_kernel, part=part), in_specs=[sme...  9 us
    pallas_call x1, Pallas kernels, order_rows(): pl.pallas_call(order_kernel, in_specs=[smem] * 3, out_specs=smem, out_sha...  8.45 us
    all_to_all x1, waiting for transfers between devices, on_device(): lax.all_to_all(blocks, 'facet', split_axis=0, concat_axis=0, tiled=True)  7.15 us
    ppermute x2, waiting for transfers between devices, on_device(): far = lax.ppermute(k0 + received[:2 * SUB], 'vis', TO_CHIP)  7.04 us
    pallas_call x2, Pallas kernels, x_sum(): pl.pallas_call(functools.partial(x_kernel, half=half), in_specs=[pl.Block...  6.59 us
    pallas_call x2, Pallas kernels, y_sum(): pl.pallas_call(functools.partial(y_kernel, half=half), grid=(NCOL // 2 //...  6.33 us
    ppermute x2, starting transfers between devices, on_device(): far = lax.ppermute(k0 + received[:2 * SUB], 'vis', TO_CHIP)  2.76 us
  transfers between devices with their start and end apart: 8, of which 5 were waited for; matrix products, arithmetic and copies ran while one was open for 0% of the time, Pallas kernels for 28%

profile of v2, /device:TPU:1, one launch (start us, length us, event | category | flops | bytes accessed | tf_op | source)
XLA Modules:
  0.0 71.8 jit_solution(12514376066456257435)
XLA Ops:
  0.0 4.2 %x_sum_a.1 = (f32[256,512]{1,0:T(8,128)}, f32[128,512]{1,0:T(8,128)}, f32[128,512]{1,0:T(8,128)}) custom-call(f32[2,256,1024]{2,1,0:T(8,128)} %facet_ref.3, bf16[4,256,256]{2,1,0:T(8,128)(2,1)} %constant.14.clone.xtab_ref, f32[128,8,256]{2,1,0:T(8,128)} %constant.15.clone.xrot_ref), custom_call_target="tpu_custom_call" | custom-call | flops 2000000000 | bytes 2000000 | tf_op jit(solution)/shard_map/x_sum_a/pallas_call | solution.py:139
  4.3 0.0 copy-start.9
  4.3 0.0 copy-start.12
  4.3 1.5 %collective-permute-start.2 = (f32[256,512]{1,0:T(8,128)}, f32[256,512]{1,0:T(8,128)S(1)}, u32[]{:S(2)}, u32[]{:S(2)}) collective-permute-start(f32[256,512]{1,0:T(8,128)} %get-tuple-element.17), channel_id=1, source_target_pairs={{0,1},{1,0},{2,3},{3,2},{4,5},{5,4},{6,7},{7,6},{8,9},{9,8},{10,11... | collective-permute-start | bytes 1572872 | tf_op jit(solution)/shard_map/ppermute | solution.py:424
  5.8 2.4 %x_sum_b.1 = (f32[256,512]{1,0:T(8,128)S(1)}, f32[128,512]{1,0:T(8,128)S(1)}, f32[128,512]{1,0:T(8,128)S(1)}) custom-call(f32[2,256,1024]{2,1,0:T(8,128)S(1)} %copy-done.4, bf16[4,256,256]{2,1,0:T(8,128)(2,1)S(1)} %copy-done.11, f32[128,8,256]{2,1,0:T(8,128)S(1)} %copy-done.10), custom_call_target="tpu_custom_call" | custom-call | flops 2000000000 | bytes 2000000 | tf_op jit(solution)/shard_map/x_sum_b/pallas_call | solution.py:139
  8.2 0.1 collective-permute-start
  8.3 0.0 collective-permute-done.2.refs_1_
  8.3 1.4 %collective-permute-start.3 = (f32[128,512]{1,0:T(8,128)S(1)}, f32[128,512]{1,0:T(8,128)S(1)}, u32[]{:S(2)}, u32[]{:S(2)}) collective-permute-start(f32[128,512]{1,0:T(8,128)S(1)} %slice_add_fusion), channel_id=1, source_target_pairs={{0,2},{2,0},{1,3},{3,1},{4,6},{6,4},{5,7},{7,5},{8,10},{10,8},{9,1... | collective-permute-start | bytes 786440 | tf_op jit(solution)/shard_map/ppermute | solution.py:425
  9.7 0.4 collective-permute-done.refs_1_
  10.2 1.4 %collective-permute-start.1 = (f32[128,512]{1,0:T(8,128)S(1)}, f32[128,512]{1,0:T(8,128)S(1)}, u32[]{:S(2)}, u32[]{:S(2)}) collective-permute-start(f32[128,512]{1,0:T(8,128)S(1)} %slice_add_fusion.1), channel_id=1, source_target_pairs={{0,2},{2,0},{1,3},{3,1},{4,6},{6,4},{5,7},{7,5},{8,10},{10,8},{9,1... | collective-permute-start | bytes 786440 | tf_op jit(solution)/shard_map/ppermute | solution.py:425
  11.6 4.2 %collective-permute-done.3.refs_2_ = f32[128,512]{1,0:T(8,128)S(1)} collective-permute-done((f32[128,512]{1,0:T(8,128)S(1)}, f32[128,512]{1,0:T(8,128)S(1)}, u32[]{:S(2)}, u32[]{:S(2)}) %collective-permute-start.3) | collective-permute-done | bytes 262176 | tf_op jit(solution)/shard_map/ppermute | solution.py:425
  15.8 2.8 %y_sum_a.1.refs_5_ = f32[32,64,128]{2,1,0:T(8,128)S(1)} custom-call(f32[128,512]{1,0:T(8,128)S(1)} %copy-done.13, f32[256,512]{1,0:T(8,128)S(1)} %collective-permute-done.2.refs_1_, f32[128,512]{1,0:T(8,128)S(1)} %collective-permute-done.3.refs_2_, bf16[16,2,256,256]{3,2,1,0:T(8,128)(2,1)S(1)} %copy-done.9, f32[8,2048]{1,0:T(8,128)S(1)} %copy-done.12), custom_call_target="tpu_custom_call" | custom-call | flops 3000000000 | bytes 6000000 | tf_op jit(solution)/shard_map/y_sum_a/pallas_call | solution.py:200
  18.6 2.8 %collective-permute-done.1.refs_2_ = f32[128,512]{1,0:T(8,128)S(1)} collective-permute-done((f32[128,512]{1,0:T(8,128)S(1)}, f32[128,512]{1,0:T(8,128)S(1)}, u32[]{:S(2)}, u32[]{:S(2)}) %collective-permute-start.1) | collective-permute-done | bytes 262176 | tf_op jit(solution)/shard_map/ppermute | solution.py:425
  21.4 0.0 copy-start.2
  21.5 0.0 copy-start.3
  21.5 3.5 %y_sum_b.1 = f32[32,64,128]{2,1,0:T(8,128)} custom-call(f32[128,512]{1,0:T(8,128)S(1)} %get-tuple-element.13.refs_0_, f32[256,512]{1,0:T(8,128)S(1)} %collective-permute-done.refs_1_, f32[128,512]{1,0:T(8,128)S(1)} %collective-permute-done.1.refs_2_, bf16[16,2,256,256]{3,2,1,0:T(8,128)(2,1)S(1)} %copy-done.9, f32[8,2048]{1,0:T(8,128)S(1)} %copy-done.12, ...), custom_call_target="tpu_custom_call" | custom-call | flops 3000000000 | bytes 6000000 | tf_op jit(solution)/shard_map/y_sum_b/pallas_call | solution.py:200
  25.0 10.7 %all-to-all-start = ((f32[32,64,128]{2,1,0:T(8,128)}), f32[32,64,128]{2,1,0:T(8,128)S(1)}, u32[]{:S(2)}, u32[]{:S(2)}) async-start(f32[32,64,128]{2,1,0:T(8,128)} %y_sum_b.1), calls=%async_computation | async-start | bytes 2097152 | tf_op jit(solution)/shard_map/all_to_all | solution.py:430
  36.4 8.4 %order_rows.1.order_ref = s32[688]{0:T(1024)S(1)} custom-call(s32[1,1]{1,0:T(1,128)S(6)} %copy.15.counts_ref, s32[1,1,512]{2,1,0:T(1,128)S(1)} %copy-done.8, s32[1,1,512]{2,1,0:T(1,128)S(1)} %bitcast.3), custom_call_target="tpu_custom_call" | custom-call | flops 20000000 | bytes 20000000 | tf_op jit(solution)/shard_map/order_rows/pallas_call | solution.py:277
  44.9 7.1 %all-to-all-done.blocks_ref = f32[32,64,128]{2,1,0:T(8,128)S(1)} async-done(((f32[32,64,128]{2,1,0:T(8,128)}), f32[32,64,128]{2,1,0:T(8,128)S(1)}, u32[]{:S(2)}, u32[]{:S(2)}) %all-to-all-start) | async-done | bytes 1048608 | tf_op jit(solution)/shard_map/all_to_all | solution.py:430
  52.0 0.0 copy-done
  52.0 1.8 %make_planes.1.planes_ref = bf16[8,128,256]{2,1,0:T(8,128)(2,1)S(1)} custom-call(s32[4,8]{1,0:T(4,128)S(1)} %bitcast.2, f32[32,64,128]{2,1,0:T(8,128)S(1)} %all-to-all-done.blocks_ref, f32[2,64,512]{2,1,0:T(8,128)S(1)} %copy-done, f32[128,128]{1,0:T(8,128)S(1)} %copy-done.2, f32[128,256]{1,0:T(8,128)S(1)} %copy-done.1), custom_call_target="tpu_custom_call" | custom-call | tf_op jit(solution)/shard_map/make_planes/pallas_call | solution.py:315
  53.8 2.6 %degrid_cross.1 = f32[256,256]{1,0:T(8,128)S(1)} custom-call(s32[688]{0:T(1024)S(1)} %order_rows.1.order_ref, s32[1,1,512]{2,1,0:T(1,128)S(1)} %copy-done.8, bf16[8,128,256]{2,1,0:T(8,128)(2,1)S(1)} %make_planes.1.planes_ref, s32[2,1,1,512,128]{4,3,2,1,0:T(8,128)S(1)} %copy-done.5, f32[2,1,1,512,128]{4,3,2,1,0:T(8,128)S(1)} %copy-done.6), custom_call_target="tpu_custom_call" | custom-call | flops 2500000000 | bytes 2000000 | tf_op jit(solution)/shard_map/degrid_cross/pallas_call | solution.py:378
  56.5 1.9 %collective-permute-start.4 = (f32[256,256]{1,0:T(8,128)S(1)}, f32[256,256]{1,0:T(8,128)S(1)}, u32[]{:S(2)}, u32[]{:S(2)}) collective-permute-start(f32[256,256]{1,0:T(8,128)S(1)} %degrid_cross.1), channel_id=1, source_target_pairs={{0,3},{3,0},{1,2},{2,1},{4,7},{7,4},{5,6},{6,5},{8,11},{11,8},{9,1... | collective-permute-start | bytes 786440 | tf_op jit(solution)/shard_map/ppermute | solution.py:435
  58.3 1.1 %degrid_chip.1 = f32[256,256]{1,0:T(8,128)S(1)} custom-call(s32[688]{0:T(1024)S(1)} %order_rows.1.order_ref, s32[1,1,512]{2,1,0:T(1,128)S(1)} %copy-done.8, bf16[8,128,256]{2,1,0:T(8,128)(2,1)S(1)} %make_planes.1.planes_ref, s32[2,1,1,512,128]{4,3,2,1,0:T(8,128)S(1)} %copy-done.5, f32[2,1,1,512,128]{4,3,2,1,0:T(8,128)S(1)} %copy-done.6), custom_call_target="tpu_custom_call" | custom-call | flops 2500000000 | bytes 2000000 | tf_op jit(solution)/shard_map/degrid_chip/pallas_call | solution.py:378
  59.5 1.7 %collective-permute-start.6 = (f32[256,256]{1,0:T(8,128)S(1)}, f32[256,256]{1,0:T(8,128)S(1)}, u32[]{:S(2)}, u32[]{:S(2)}) collective-permute-start(f32[256,256]{1,0:T(8,128)S(1)} %degrid_chip.1), channel_id=1, source_target_pairs={{0,2},{2,0},{1,3},{3,1},{4,6},{6,4},{5,7},{7,5},{8,10},{10,8},{9,1... | collective-permute-start | bytes 786440 | tf_op jit(solution)/shard_map/ppermute | solution.py:436
  61.1 3.6 %degrid_core.1 = f32[256,256]{1,0:T(8,128)S(1)} custom-call(s32[688]{0:T(1024)S(1)} %order_rows.1.order_ref, s32[1,1,512]{2,1,0:T(1,128)S(1)} %copy-done.8, bf16[8,128,256]{2,1,0:T(8,128)(2,1)S(1)} %make_planes.1.planes_ref, s32[2,1,1,512,128]{4,3,2,1,0:T(8,128)S(1)} %copy-done.5, f32[2,1,1,512,128]{4,3,2,1,0:T(8,128)S(1)} %copy-done.6), custom_call_target="tpu_custom_call" | custom-call | flops 2500000000 | bytes 2000000 | tf_op jit(solution)/shard_map/degrid_core/pallas_call | solution.py:378
  64.8 0.0 collective-permute-done.4.cross_ref
  64.8 2.1 %collective-permute-start.5 = (f32[256,256]{1,0:T(8,128)S(1)}, f32[256,256]{1,0:T(8,128)S(1)}, u32[]{:S(2)}, u32[]{:S(2)}) collective-permute-start(f32[256,256]{1,0:T(8,128)S(1)} %degrid_core.1), channel_id=1, source_target_pairs={{0,1},{1,0},{2,3},{3,2},{4,5},{5,4},{6,7},{7,6},{8,9},{9,8},{10,11... | collective-permute-start | bytes 786440 | tf_op jit(solution)/shard_map/ppermute | solution.py:438
  66.9 1.6 %degrid_own.1.self_ref = f32[256,256]{1,0:T(8,128)S(1)} custom-call(s32[688]{0:T(1024)S(1)} %order_rows.1.order_ref, s32[1,1,512]{2,1,0:T(1,128)S(1)} %copy-done.8, bf16[8,128,256]{2,1,0:T(8,128)(2,1)S(1)} %make_planes.1.planes_ref, s32[2,1,1,512,128]{4,3,2,1,0:T(8,128)S(1)} %copy-done.5, f32[2,1,1,512,128]{4,3,2,1,0:T(8,128)S(1)} %copy-done.6), custom_call_target="tpu_custom_call" | custom-call | flops 2500000000 | bytes 2000000 | tf_op jit(solution)/shard_map/degrid_own/pallas_call | solution.py:378
  68.5 2.3 %collective-permute-done.6.chip_ref = f32[256,256]{1,0:T(8,128)S(1)} collective-permute-done((f32[256,256]{1,0:T(8,128)S(1)}, f32[256,256]{1,0:T(8,128)S(1)}, u32[]{:S(2)}, u32[]{:S(2)}) %collective-permute-start.6) | collective-permute-done | bytes 262176 | tf_op jit(solution)/shard_map/ppermute | solution.py:436
  70.8 0.0 collective-permute-done.5.core_ref
  70.8 1.0 %gather_rows.1 = f32[1,1,4,256,256]{4,3,2,1,0:T(8,128)} custom-call(f32[256,256]{1,0:T(8,128)S(1)} %degrid_own.1.self_ref, f32[256,256]{1,0:T(8,128)S(1)} %collective-permute-done.5.core_ref, f32[256,256]{1,0:T(8,128)S(1)} %collective-permute-done.6.chip_ref, f32[256,256]{1,0:T(8,128)S(1)} %collective-permute-done.4.cross_ref), custom_call_target="tpu_custom_call" | custom-call | tf_op jit(solution)/shard_map/gather_rows/pallas_call | solution.py:403
  (27 shorter events, 0.1 us)
Async XLA Ops:
  0.0 5.8 %copy-start.11 = (bf16[4,256,256]{2,1,0:T(8,128)(2,1)S(1)}, bf16[4,256,256]{2,1,0:T(8,128)(2,1)}, u32[]{:S(2)}) copy-start(bf16[4,256,256]{2,1,0:T(8,128)(2,1)} %constant.14.clone.xtab_ref) | copy-start | bytes 1572868
  0.0 5.8 %copy-start.10 = (f32[128,8,256]{2,1,0:T(8,128)S(1)}, f32[128,8,256]{2,1,0:T(8,128)}, u32[]{:S(2)}) copy-start(f32[128,8,256]{2,1,0:T(8,128)} %constant.15.clone.xrot_ref) | copy-start | bytes 3145732
  0.0 5.8 %copy-start.4 = (f32[2,256,1024]{2,1,0:T(8,128)S(1)}, f32[2,256,1024]{2,1,0:T(8,128)}, u32[]{:S(2)}) copy-start(f32[2,256,1024]{2,1,0:T(8,128)} %facet_ref.3) | copy-start | bytes 6291460
  4.2 4.0 %copy-start.14 = (f32[128,512]{1,0:T(8,128)S(1)}, f32[128,512]{1,0:T(8,128)}, u32[]{:S(2)}) copy-start(f32[128,512]{1,0:T(8,128)} %get-tuple-element.18) | copy-start | bytes 786436
  4.3 11.6 %copy-start.9 = (bf16[16,2,256,256]{3,2,1,0:T(8,128)(2,1)S(1)}, bf16[16,2,256,256]{3,2,1,0:T(8,128)(2,1)}, u32[]{:S(2)}) copy-start(bf16[16,2,256,256]{3,2,1,0:T(8,128)(2,1)} %constant.16.clone.refs_3_) | copy-start | bytes 12582916
  4.3 11.5 %copy-start.12 = (f32[8,2048]{1,0:T(8,128)S(1)}, f32[8,2048]{1,0:T(8,128)}, u32[]{:S(2)}) copy-start(f32[8,2048]{1,0:T(8,128)} %constant.17.clone.refs_4_) | copy-start | bytes 196612
  4.3 11.5 %copy-start.13 = (f32[128,512]{1,0:T(8,128)S(1)}, f32[128,512]{1,0:T(8,128)}, u32[]{:S(2)}) copy-start(f32[128,512]{1,0:T(8,128)} %get-tuple-element.16.refs_0_) | copy-start | bytes 786436
  4.3 4.0 %collective-permute-start.2 = (f32[256,512]{1,0:T(8,128)}, f32[256,512]{1,0:T(8,128)S(1)}, u32[]{:S(2)}, u32[]{:S(2)}) collective-permute-start(f32[256,512]{1,0:T(8,128)} %get-tuple-element.17), channel_id=1, source_target_pairs={{0,1},{1,0},{2,3},{3,2},{4,5},{5,4},{6,7},{7,6},{8,9},{9,8},{10,11... | collective-permute-start | bytes 1572872 | tf_op jit(solution)/shard_map/ppermute | solution.py:424
  8.2 2.0 %collective-permute-start = (f32[256,512]{1,0:T(8,128)S(1)}, f32[256,512]{1,0:T(8,128)S(1)}, u32[]{:S(2)}, u32[]{:S(2)}) collective-permute-start(f32[256,512]{1,0:T(8,128)S(1)} %get-tuple-element.14), channel_id=1, source_target_pairs={{0,1},{1,0},{2,3},{3,2},{4,5},{5,4},{6,7},{7,6},{8,9},{9,8},{10,11... | collective-permute-start | bytes 1572872 | tf_op jit(solution)/shard_map/ppermute | solution.py:424
  8.3 7.5 %collective-permute-start.3 = (f32[128,512]{1,0:T(8,128)S(1)}, f32[128,512]{1,0:T(8,128)S(1)}, u32[]{:S(2)}, u32[]{:S(2)}) collective-permute-start(f32[128,512]{1,0:T(8,128)S(1)} %slice_add_fusion), channel_id=1, source_target_pairs={{0,2},{2,0},{1,3},{3,1},{4,6},{6,4},{5,7},{7,5},{8,10},{10,8},{9,1... | collective-permute-start | bytes 786440 | tf_op jit(solution)/shard_map/ppermute | solution.py:425
  10.2 11.2 %collective-permute-start.1 = (f32[128,512]{1,0:T(8,128)S(1)}, f32[128,512]{1,0:T(8,128)S(1)}, u32[]{:S(2)}, u32[]{:S(2)}) collective-permute-start(f32[128,512]{1,0:T(8,128)S(1)} %slice_add_fusion.1), channel_id=1, source_target_pairs={{0,2},{2,0},{1,3},{3,1},{4,6},{6,4},{5,7},{7,5},{8,10},{10,8},{9,1... | collective-permute-start | bytes 786440 | tf_op jit(solution)/shard_map/ppermute | solution.py:425
  21.4 15.0 %copy-start.7 = (s32[1,1,512,1]{2,3,1,0:T(1,128)S(1)}, s32[1,1,512,1]{2,3,1,0:T(1,128)}, u32[]{:S(2)}) copy-start(s32[1,1,512,1]{2,3,1,0:T(1,128)} %param.20) | copy-start | bytes 6148
  21.4 15.0 %copy-start.8 = (s32[1,1,512]{2,1,0:T(1,128)S(1)}, s32[1,1,512]{2,1,0:T(1,128)}, u32[]{:S(2)}) copy-start(s32[1,1,512]{2,1,0:T(1,128)} %wplanes_ref.9) | copy-start | bytes 6148
  21.4 30.6 %copy-start = (f32[2,64,512]{2,1,0:T(8,128)S(1)}, f32[2,64,512]{2,1,0:T(8,128)}, u32[]{:S(2)}) copy-start(f32[2,64,512]{2,1,0:T(8,128)} %constant.18.clone.screens_ref) | copy-start | bytes 786436
  21.4 30.6 %copy-start.1 = (f32[128,256]{1,0:T(8,128)S(1)}, f32[128,256]{1,0:T(8,128)}, u32[]{:S(2)}) copy-start(f32[128,256]{1,0:T(8,128)} %constant.20.clone.right_ref) | copy-start | bytes 393220
  21.4 30.6 %copy-start.2 = (f32[128,128]{1,0:T(8,128)S(1)}, f32[128,128]{1,0:T(8,128)}, u32[]{:S(2)}) copy-start(f32[128,128]{1,0:T(8,128)} %constant.19.clone.left_ref) | copy-start | bytes 196612
  21.5 30.6 %copy-start.3 = (s32[4,1,8]{2,1,0:T(1,128)S(1)}, s32[4,1,8]{2,1,0:T(1,128)}, u32[]{:S(2)}) copy-start(s32[4,1,8]{2,1,0:T(1,128)} %param.15) | copy-start | bytes 388
  25.0 28.8 %copy-start.5 = (s32[2,1,1,512,128]{4,3,2,1,0:T(8,128)S(1)}, s32[2,1,1,512,128]{4,3,2,1,0:T(8,128)}, u32[]{:S(2)}) copy-start(s32[2,1,1,512,128]{4,3,2,1,0:T(8,128)} %offsets_ref.7) | copy-start | bytes 1572868
  25.0 28.8 %copy-start.6 = (f32[2,1,1,512,128]{4,3,2,1,0:T(8,128)S(1)}, f32[2,1,1,512,128]{4,3,2,1,0:T(8,128)}, u32[]{:S(2)}) copy-start(f32[2,1,1,512,128]{4,3,2,1,0:T(8,128)} %frac_ref.7) | copy-start | bytes 1572868
  25.0 27.0 %all-to-all-start = ((f32[32,64,128]{2,1,0:T(8,128)}), f32[32,64,128]{2,1,0:T(8,128)S(1)}, u32[]{:S(2)}, u32[]{:S(2)}) async-start(f32[32,64,128]{2,1,0:T(8,128)} %y_sum_b.1), calls=%async_computation | async-start | bytes 2097152 | tf_op jit(solution)/shard_map/all_to_all | solution.py:430
  56.5 8.3 %collective-permute-start.4 = (f32[256,256]{1,0:T(8,128)S(1)}, f32[256,256]{1,0:T(8,128)S(1)}, u32[]{:S(2)}, u32[]{:S(2)}) collective-permute-start(f32[256,256]{1,0:T(8,128)S(1)} %degrid_cross.1), channel_id=1, source_target_pairs={{0,3},{3,0},{1,2},{2,1},{4,7},{7,4},{5,6},{6,5},{8,11},{11,8},{9,1... | collective-permute-start | bytes 786440 | tf_op jit(solution)/shard_map/ppermute | solution.py:435
  59.5 11.3 %collective-permute-start.6 = (f32[256,256]{1,0:T(8,128)S(1)}, f32[256,256]{1,0:T(8,128)S(1)}, u32[]{:S(2)}, u32[]{:S(2)}) collective-permute-start(f32[256,256]{1,0:T(8,128)S(1)} %degrid_chip.1), channel_id=1, source_target_pairs={{0,2},{2,0},{1,3},{3,1},{4,6},{6,4},{5,7},{7,5},{8,10},{10,8},{9,1... | collective-permute-start | bytes 786440 | tf_op jit(solution)/shard_map/ppermute | solution.py:436
  64.8 6.1 %collective-permute-start.5 = (f32[256,256]{1,0:T(8,128)S(1)}, f32[256,256]{1,0:T(8,128)S(1)}, u32[]{:S(2)}, u32[]{:S(2)}) collective-permute-start(f32[256,256]{1,0:T(8,128)S(1)} %degrid_core.1), channel_id=1, source_target_pairs={{0,1},{1,0},{2,3},{3,2},{4,5},{5,4},{6,7},{7,6},{8,9},{9,8},{10,11... | collective-permute-start | bytes 786440 | tf_op jit(solution)/shard_map/ppermute | solution.py:438

commit v3 on v2

--- a/solution.py
+++ b/solution.py
@@ -98,30 +98,43 @@
     return jnp.dot(a, b, preferred_element_type=F32)
 
 
-def x_kernel(facet_ref, xtab_ref, xrot_ref, send_ref, k0_ref, k1_ref, rhs_ref, tab_ref, turn_ref, rot_ref, sems, *, half):
+def x_kernel(facet_ref, xtab_ref, xrot_ref, send_ref, k0_ref, k1_ref, rot_ref, *scratch, half):
     vis = lax.axis_index("vis")
     x_lo, core = vis // 2, vis % 2
-    loads = [
-        pltpu.make_async_copy(xtab_ref, tab_ref, sems.at[0]),
-        pltpu.make_async_copy(xrot_ref.at[lax.axis_index("facet") * N_VIS + vis], turn_ref, sems.at[1]),
-    ]
-    for i in range(2):
-        columns = pl.ds((2 * half + i) * YBLK, YBLK)
-        loads.append(pltpu.make_async_copy(facet_ref.at[:, :, columns], rhs_ref.at[i], sems.at[2 + i]))
-    for load in loads:
-        load.start()
-    loads[1].wait()
-    rot_ref[...] = turn_ref[...].T
-    loads[0].wait()
+    place = lax.axis_index("facet") * N_VIS + vis
+    if half == 0:
+        rhs_ref, tab_ref, turn_ref, sems = scratch
+        loads = [
+            pltpu.make_async_copy(xtab_ref, tab_ref, sems.at[0]),
+            pltpu.make_async_copy(xrot_ref.at[place], turn_ref, sems.at[1]),
+        ]
+        for i in range(2):
+            loads.append(
+                pltpu.make_async_copy(facet_ref.at[i, :, pl.ds(0, FP // 2)], rhs_ref.at[i], sems.at[2 + i])
+            )
+        for load in loads:
+            load.start()
+        loads[1].wait()
+        rot_ref[...] = turn_ref[...].T
+        loads[0].wait()
+    else:
+        tab_ref = xtab_ref
+        rot_ref[...] = xrot_ref[place].T
     order = row_order(x_lo, core)
     full = jnp.concatenate([tab_ref[r] for r in order], 0)
     high = jnp.concatenate([tab_ref[r, : 2 * SUB] for r in order], 0)
     outs = (send_ref.at[: 2 * SUB], send_ref.at[2 * SUB :], k0_ref, k1_ref)
     for block in range(2):
-        loads[2 + block].wait()
+        if half == 0 and block == 0:
+            loads[2].wait()
+            loads[3].wait()
         a = []
         for part in range(2):
-            hi, lo = split(rhs_ref[block, part])
+            if half == 0:
+                values = rhs_ref[part, :, block * YBLK : (block + 1) * YBLK]
+            else:
+                values = facet_ref[part, :, (2 + block) * YBLK : (3 + block) * YBLK]
+            hi, lo = split(values)
             both = dot(full, hi).reshape(N_VIS, 2, 2 * SUB, YBLK)
             a.append(both[:, 0] + both[:, 1] + dot(high, lo).reshape(N_VIS, 2 * SUB, YBLK))
         for i, out in enumerate(outs):
@@ -136,25 +149,22 @@
 def x_sum(half, facet_image, xtab, xrot):
     vmem = pl.BlockSpec(memory_space=pltpu.VMEM)
     kept = jax.ShapeDtypeStruct((2 * SUB, FP // 2), F32)
+    copied = [
+        pltpu.VMEM((2, XROWS, FP // 2), F32),
+        pltpu.VMEM(xtab.shape, BF16),
+        pltpu.VMEM(xrot.shape[1:], F32),
+        pltpu.SemaphoreType.DMA((4,)),
+    ]
     return pl.pallas_call(
         functools.partial(x_kernel, half=half),
-        in_specs=[pl.BlockSpec(memory_space=pltpu.HBM)] * 3,
+        in_specs=[pl.BlockSpec(memory_space=pltpu.HBM) if half == 0 else vmem] * 3,
         out_specs=[vmem] * 3,
         out_shape=[jax.ShapeDtypeStruct((4 * SUB, FP // 2), F32), kept, kept],
-        scratch_shapes=[
-            pltpu.VMEM((2, 2, XROWS, YBLK), F32),
-            pltpu.VMEM(xtab.shape, BF16),
-            pltpu.VMEM(xrot.shape[1:], F32),
-            pltpu.VMEM((N_VIS * SUB, 8), F32),
-            pltpu.SemaphoreType.DMA((4,)),
-        ],
+        scratch_shapes=[pltpu.VMEM((N_VIS * SUB, 8), F32)] + (copied if half == 0 else []),
         compiler_params=pltpu.CompilerParams(vmem_limit_bytes=(60, 20)[half] * 1024 * 1024),
         cost_estimate=pl.CostEstimate(flops=2_000_000_000, bytes_accessed=2_000_000, transcendentals=0),
         name="x_sum_" + "ab"[half],
     )(facet_image, xtab, xrot)
-
-
-PAIRS = 4
 
 
 def y_kernel(*refs, half):
@@ -163,15 +173,15 @@
     else:
         kept_ref, near_ref, far_ref, ytab_ref, yrot_ref, first_ref, out_ref, lhs_ref = refs
 
-    @pl.when(pl.program_id(0) == 0)
-    def _():
-        hi, lo = split(kept_ref[...] + near_ref[...] + far_ref[...])
-        for y in range(2):
-            now = slice(y * YBLK, (y + 1) * YBLK)
-            lhs_ref[y * 128 : (y + 1) * 128] = jnp.concatenate([hi[:, now], lo[:, now], hi[:, now]], 1)
+    hi, lo = split(kept_ref[...] + near_ref[2 * SUB :] + far_ref[...])
+    lhs = []
+    for y in range(2):
+        now = slice(y * YBLK, (y + 1) * YBLK)
+        lhs.append(jnp.concatenate([hi[:, now], lo[:, now], hi[:, now]], 1))
+    lhs_ref[...] = jnp.concatenate(lhs, 0)
 
     left_half = lax.broadcasted_iota(jnp.int32, (64, 128), 1) < 64
-    for w in range(PAIRS):
+    for w in range(NCOL // 2):
         part = dot(lhs_ref[...], jnp.concatenate([ytab_ref[w, 0], ytab_ref[w, 0], ytab_ref[w, 1]], 0))
         re = im = None
         for y in range(2):
@@ -195,20 +205,11 @@
 
 
 def y_sum(half, kept, received, far, ytab, yrot, *first):
-    whole = pl.BlockSpec((2 * SUB, FP // 2), lambda i: (0, 0))
-    columns = pl.BlockSpec((2 * PAIRS, SUB, 2 * SUB), lambda i: (i, 0, 0))
+    vmem = pl.BlockSpec(memory_space=pltpu.VMEM)
     return pl.pallas_call(
         functools.partial(y_kernel, half=half),
-        grid=(NCOL // 2 // PAIRS,),
-        in_specs=[
-            whole,
-            pl.BlockSpec((2 * SUB, FP // 2), lambda i: (1, 0)),
-            whole,
-            pl.BlockSpec((PAIRS, 2, YBLK, 256), lambda i: (i, 0, 0, 0)),
-            pl.BlockSpec((8, 128 * PAIRS), lambda i: (0, i)),
-        ]
-        + [columns] * len(first),
-        out_specs=columns,
+        in_specs=[vmem] * (5 + len(first)),
+        out_specs=vmem,
         out_shape=jax.ShapeDtypeStruct((NCOL, SUB, 2 * SUB), F32),
         scratch_shapes=[pltpu.VMEM((2 * 128, 3 * YBLK), BF16)],
         compiler_params=pltpu.CompilerParams(vmem_limit_bytes=VMEM_LIMIT),

time: 72.7 us -> 70.3 us (0.967); the launches traced: 71.8 us -> 70.9 us
  Pallas kernels: 33.1 us -> 27 us
  waiting for transfers between devices: 17 us -> 19.8 us
  starting transfers between devices: 20.7 us -> 23.1 us
    ppermute x1, starting transfers between devices: 1.66 us -> 4.17 us  [on_device(): from_chip = lax.ppermute(to_chip, 'vis', TO_CHIP)]
    pallas_call x4, Pallas kernels: 9 us -> 6.54 us  [degrid(): pl.pallas_call(functools.partial(degrid_kernel, part=part), in_specs=[sme...]
    pallas_call x2, Pallas kernels: 6.59 us -> 4.51 us  [x_sum(): pl.pallas_call(functools.partial(x_kernel, half=half), in_specs=[pl.Block...]
    ppermute x2, waiting for transfers between devices: 7.04 us -> 8.59 us  [on_device(): far = lax.ppermute(k0 + received[:2 * SUB], 'vis', TO_CHIP)]
    pallas_call x2, Pallas kernels: 6.33 us -> 4.79 us  [y_sum(): pl.pallas_call(functools.partial(y_kernel, half=half), in_specs=[vmem] *...]
    ppermute x1, waiting for transfers between devices: 2.32 us -> 3.52 us  [on_device(): from_chip = lax.ppermute(to_chip, 'vis', TO_CHIP)]
  transfers between devices with their start and end apart: 8 -> 8, of which waited for: 5 -> 5; matrix products, arithmetic and copies ran while one was open for 0% -> 0% of each run, Pallas kernels for 28% -> 23%
where the time goes in v3:
time: 70.3 us; the launch traced here: 70.9 us
  Pallas kernels  27 us (38%)
  starting transfers between devices  23.1 us (33%)
  waiting for transfers between devices  19.8 us (28%)
  between operations  0.86 us (1%)
    all_to_all x1, starting transfers between devices, on_device(): lax.all_to_all(blocks, 'facet', split_axis=0, concat_axis=0, tiled=True)  10.7 us
    ppermute x2, waiting for transfers between devices, on_device(): far = lax.ppermute(k0 + received[:2 * SUB], 'vis', TO_CHIP)  8.59 us
    pallas_call x1, Pallas kernels, order_rows(): pl.pallas_call(order_kernel, in_specs=[smem] * 3, out_specs=smem, out_sha...  8.45 us
    all_to_all x1, waiting for transfers between devices, on_device(): lax.all_to_all(blocks, 'facet', split_axis=0, concat_axis=0, tiled=True)  7.17 us
    pallas_call x4, Pallas kernels, degrid(): pl.pallas_call(functools.partial(degrid_kernel, part=part), in_specs=[sme...  6.54 us
    pallas_call x2, Pallas kernels, y_sum(): pl.pallas_call(functools.partial(y_kernel, half=half), in_specs=[vmem] *...  4.79 us
    pallas_call x2, Pallas kernels, x_sum(): pl.pallas_call(functools.partial(x_kernel, half=half), in_specs=[pl.Block...  4.51 us
    ppermute x1, starting transfers between devices, on_device(): from_chip = lax.ppermute(to_chip, 'vis', TO_CHIP)  4.17 us
  transfers between devices with their start and end apart: 8, of which 5 were waited for; matrix products, arithmetic and copies ran while one was open for 0% of the time, Pallas kernels for 23%

profile of v3, /device:TPU:1, one launch (start us, length us, event | category | flops | bytes accessed | tf_op | source)
XLA Modules:
  0.0 70.9 jit_solution(16787150920558158902)
XLA Ops:
  0.0 3.4 %x_sum_a.1 = (f32[256,512]{1,0:T(8,128)}, f32[128,512]{1,0:T(8,128)}, f32[128,512]{1,0:T(8,128)}) custom-call(f32[2,256,1024]{2,1,0:T(8,128)} %facet_ref.3, bf16[4,256,256]{2,1,0:T(8,128)(2,1)} %constant.14.clone.xtab_ref, f32[128,8,256]{2,1,0:T(8,128)} %constant.15.clone.xrot_ref), custom_call_target="tpu_custom_call" | custom-call | flops 2000000000 | bytes 2000000 | tf_op jit(solution)/shard_map/x_sum_a/pallas_call | solution.py:158
  3.5 0.0 copy-start.9
  3.5 0.0 copy-start.12
  3.5 1.5 %collective-permute-start.2 = (f32[256,512]{1,0:T(8,128)}, f32[256,512]{1,0:T(8,128)S(1)}, u32[]{:S(2)}, u32[]{:S(2)}) collective-permute-start(f32[256,512]{1,0:T(8,128)} %get-tuple-element.17), channel_id=1, source_target_pairs={{0,1},{1,0},{2,3},{3,2},{4,5},{5,4},{6,7},{7,6},{8,9},{9,8},{10,11... | collective-permute-start | bytes 1572872 | tf_op jit(solution)/shard_map/ppermute | solution.py:425
  5.0 0.0 copy-done.11
  5.0 1.1 %x_sum_b.1 = (f32[256,512]{1,0:T(8,128)S(1)}, f32[128,512]{1,0:T(8,128)S(1)}, f32[128,512]{1,0:T(8,128)S(1)}) custom-call(f32[2,256,1024]{2,1,0:T(8,128)S(1)} %copy-done.4, bf16[4,256,256]{2,1,0:T(8,128)(2,1)S(1)} %copy-done.11, f32[128,8,256]{2,1,0:T(8,128)S(1)} %copy-done.10), custom_call_target="tpu_custom_call" | custom-call | flops 2000000000 | bytes 2000000 | tf_op jit(solution)/shard_map/x_sum_b/pallas_call | solution.py:158
  6.1 0.1 collective-permute-start
  6.2 0.6 collective-permute-done.2.refs_1_
  6.8 1.4 %collective-permute-start.3 = (f32[128,512]{1,0:T(8,128)S(1)}, f32[128,512]{1,0:T(8,128)S(1)}, u32[]{:S(2)}, u32[]{:S(2)}) collective-permute-start(f32[128,512]{1,0:T(8,128)S(1)} %slice_add_fusion), channel_id=1, source_target_pairs={{0,2},{2,0},{1,3},{3,1},{4,6},{6,4},{5,7},{7,5},{8,10},{10,8},{9,1... | collective-permute-start | bytes 786440 | tf_op jit(solution)/shard_map/ppermute | solution.py:426
  8.2 0.0 collective-permute-done.refs_1_
  8.2 1.3 %collective-permute-start.1 = (f32[128,512]{1,0:T(8,128)S(1)}, f32[128,512]{1,0:T(8,128)S(1)}, u32[]{:S(2)}, u32[]{:S(2)}) collective-permute-start(f32[128,512]{1,0:T(8,128)S(1)} %slice_add_fusion.1), channel_id=1, source_target_pairs={{0,2},{2,0},{1,3},{3,1},{4,6},{6,4},{5,7},{7,5},{8,10},{10,8},{9,1... | collective-permute-start | bytes 786440 | tf_op jit(solution)/shard_map/ppermute | solution.py:426
  9.5 4.9 %collective-permute-done.3.refs_2_ = f32[128,512]{1,0:T(8,128)S(1)} collective-permute-done((f32[128,512]{1,0:T(8,128)S(1)}, f32[128,512]{1,0:T(8,128)S(1)}, u32[]{:S(2)}, u32[]{:S(2)}) %collective-permute-start.3) | collective-permute-done | bytes 262176 | tf_op jit(solution)/shard_map/ppermute | solution.py:426
  14.4 1.9 %y_sum_a.1.refs_5_ = f32[32,64,128]{2,1,0:T(8,128)S(1)} custom-call(f32[128,512]{1,0:T(8,128)S(1)} %copy-done.13, f32[256,512]{1,0:T(8,128)S(1)} %collective-permute-done.2.refs_1_, f32[128,512]{1,0:T(8,128)S(1)} %collective-permute-done.3.refs_2_, bf16[16,2,256,256]{3,2,1,0:T(8,128)(2,1)S(1)} %copy-done.9, f32[8,2048]{1,0:T(8,128)S(1)} %copy-done.12), custom_call_target="tpu_custom_call" | custom-call | flops 3000000000 | bytes 6000000 | tf_op jit(solution)/shard_map/y_sum_a/pallas_call | solution.py:209
  16.3 3.7 %collective-permute-done.1.refs_2_ = f32[128,512]{1,0:T(8,128)S(1)} collective-permute-done((f32[128,512]{1,0:T(8,128)S(1)}, f32[128,512]{1,0:T(8,128)S(1)}, u32[]{:S(2)}, u32[]{:S(2)}) %collective-permute-start.1) | collective-permute-done | bytes 262176 | tf_op jit(solution)/shard_map/ppermute | solution.py:426
  20.0 0.0 copy-start.2
  20.0 0.0 copy-start.3
  20.0 2.9 %y_sum_b.1 = f32[32,64,128]{2,1,0:T(8,128)} custom-call(f32[128,512]{1,0:T(8,128)S(1)} %get-tuple-element.13.refs_0_, f32[256,512]{1,0:T(8,128)S(1)} %collective-permute-done.refs_1_, f32[128,512]{1,0:T(8,128)S(1)} %collective-permute-done.1.refs_2_, bf16[16,2,256,256]{3,2,1,0:T(8,128)(2,1)S(1)} %copy-done.9, f32[8,2048]{1,0:T(8,128)S(1)} %copy-done.12, ...), custom_call_target="tpu_custom_call" | custom-call | flops 3000000000 | bytes 6000000 | tf_op jit(solution)/shard_map/y_sum_b/pallas_call | solution.py:209
  22.9 10.7 %all-to-all-start = ((f32[32,64,128]{2,1,0:T(8,128)}), f32[32,64,128]{2,1,0:T(8,128)S(1)}, u32[]{:S(2)}, u32[]{:S(2)}) async-start(f32[32,64,128]{2,1,0:T(8,128)} %y_sum_b.1), calls=%async_computation | async-start | bytes 2097152 | tf_op jit(solution)/shard_map/all_to_all | solution.py:431
  34.3 8.4 %order_rows.1.order_ref = s32[688]{0:T(1024)S(1)} custom-call(s32[1,1]{1,0:T(1,128)S(6)} %copy.15.counts_ref, s32[1,1,512]{2,1,0:T(1,128)S(1)} %copy-done.8, s32[1,1,512]{2,1,0:T(1,128)S(1)} %bitcast.3), custom_call_target="tpu_custom_call" | custom-call | flops 20000000 | bytes 20000000 | tf_op jit(solution)/shard_map/order_rows/pallas_call | solution.py:278
  42.8 7.2 %all-to-all-done.blocks_ref = f32[32,64,128]{2,1,0:T(8,128)S(1)} async-done(((f32[32,64,128]{2,1,0:T(8,128)}), f32[32,64,128]{2,1,0:T(8,128)S(1)}, u32[]{:S(2)}, u32[]{:S(2)}) %all-to-all-start) | async-done | bytes 1048608 | tf_op jit(solution)/shard_map/all_to_all | solution.py:431
  50.0 1.8 %make_planes.1.planes_ref = bf16[8,128,256]{2,1,0:T(8,128)(2,1)S(1)} custom-call(s32[4,8]{1,0:T(4,128)S(1)} %bitcast.2, f32[32,64,128]{2,1,0:T(8,128)S(1)} %all-to-all-done.blocks_ref, f32[2,64,512]{2,1,0:T(8,128)S(1)} %copy-done, f32[128,128]{1,0:T(8,128)S(1)} %copy-done.2, f32[128,256]{1,0:T(8,128)S(1)} %copy-done.1), custom_call_target="tpu_custom_call" | custom-call | tf_op jit(solution)/shard_map/make_planes/pallas_call | solution.py:316
  51.8 1.6 %degrid_cross.1 = f32[256,256]{1,0:T(8,128)S(1)} custom-call(s32[688]{0:T(1024)S(1)} %order_rows.1.order_ref, s32[1,1,512]{2,1,0:T(1,128)S(1)} %copy-done.8, bf16[8,128,256]{2,1,0:T(8,128)(2,1)S(1)} %make_planes.1.planes_ref, s32[2,1,1,512,128]{4,3,2,1,0:T(8,128)S(1)} %copy-done.5, f32[2,1,1,512,128]{4,3,2,1,0:T(8,128)S(1)} %copy-done.6), custom_call_target="tpu_custom_call" | custom-call | flops 2500000000 | bytes 2000000 | tf_op jit(solution)/shard_map/degrid_cross/pallas_call | solution.py:379
  53.4 2.3 %collective-permute-start.4 = (f32[256,256]{1,0:T(8,128)S(1)}, f32[256,256]{1,0:T(8,128)S(1)}, u32[]{:S(2)}, u32[]{:S(2)}) collective-permute-start(f32[256,256]{1,0:T(8,128)S(1)} %degrid_cross.1), channel_id=1, source_target_pairs={{0,3},{3,0},{1,2},{2,1},{4,7},{7,4},{5,6},{6,5},{8,11},{11,8},{9,1... | collective-permute-start | bytes 786440 | tf_op jit(solution)/shard_map/ppermute | solution.py:436
  55.8 2.1 %degrid_chip.1 = f32[256,256]{1,0:T(8,128)S(1)} custom-call(s32[688]{0:T(1024)S(1)} %order_rows.1.order_ref, s32[1,1,512]{2,1,0:T(1,128)S(1)} %copy-done.8, bf16[8,128,256]{2,1,0:T(8,128)(2,1)S(1)} %make_planes.1.planes_ref, s32[2,1,1,512,128]{4,3,2,1,0:T(8,128)S(1)} %copy-done.5, f32[2,1,1,512,128]{4,3,2,1,0:T(8,128)S(1)} %copy-done.6), custom_call_target="tpu_custom_call" | custom-call | flops 2500000000 | bytes 2000000 | tf_op jit(solution)/shard_map/degrid_chip/pallas_call | solution.py:379
  57.9 4.2 %collective-permute-start.6 = (f32[256,256]{1,0:T(8,128)S(1)}, f32[256,256]{1,0:T(8,128)S(1)}, u32[]{:S(2)}, u32[]{:S(2)}) collective-permute-start(f32[256,256]{1,0:T(8,128)S(1)} %degrid_chip.1), channel_id=1, source_target_pairs={{0,2},{2,0},{1,3},{3,1},{4,6},{6,4},{5,7},{7,5},{8,10},{10,8},{9,1... | collective-permute-start | bytes 786440 | tf_op jit(solution)/shard_map/ppermute | solution.py:437
  62.1 1.6 %degrid_core.1 = f32[256,256]{1,0:T(8,128)S(1)} custom-call(s32[688]{0:T(1024)S(1)} %order_rows.1.order_ref, s32[1,1,512]{2,1,0:T(1,128)S(1)} %copy-done.8, bf16[8,128,256]{2,1,0:T(8,128)(2,1)S(1)} %make_planes.1.planes_ref, s32[2,1,1,512,128]{4,3,2,1,0:T(8,128)S(1)} %copy-done.5, f32[2,1,1,512,128]{4,3,2,1,0:T(8,128)S(1)} %copy-done.6), custom_call_target="tpu_custom_call" | custom-call | flops 2500000000 | bytes 2000000 | tf_op jit(solution)/shard_map/degrid_core/pallas_call | solution.py:379
  63.7 0.0 collective-permute-done.4.cross_ref
  63.7 1.6 %collective-permute-start.5 = (f32[256,256]{1,0:T(8,128)S(1)}, f32[256,256]{1,0:T(8,128)S(1)}, u32[]{:S(2)}, u32[]{:S(2)}) collective-permute-start(f32[256,256]{1,0:T(8,128)S(1)} %degrid_core.1), channel_id=1, source_target_pairs={{0,1},{1,0},{2,3},{3,2},{4,5},{5,4},{6,7},{7,6},{8,9},{9,8},{10,11... | collective-permute-start | bytes 786440 | tf_op jit(solution)/shard_map/ppermute | solution.py:439
  65.3 1.1 %degrid_own.1.self_ref = f32[256,256]{1,0:T(8,128)S(1)} custom-call(s32[688]{0:T(1024)S(1)} %order_rows.1.order_ref, s32[1,1,512]{2,1,0:T(1,128)S(1)} %copy-done.8, bf16[8,128,256]{2,1,0:T(8,128)(2,1)S(1)} %make_planes.1.planes_ref, s32[2,1,1,512,128]{4,3,2,1,0:T(8,128)S(1)} %copy-done.5, f32[2,1,1,512,128]{4,3,2,1,0:T(8,128)S(1)} %copy-done.6), custom_call_target="tpu_custom_call" | custom-call | flops 2500000000 | bytes 2000000 | tf_op jit(solution)/shard_map/degrid_own/pallas_call | solution.py:379
  66.4 3.5 %collective-permute-done.6.chip_ref = f32[256,256]{1,0:T(8,128)S(1)} collective-permute-done((f32[256,256]{1,0:T(8,128)S(1)}, f32[256,256]{1,0:T(8,128)S(1)}, u32[]{:S(2)}, u32[]{:S(2)}) %collective-permute-start.6) | collective-permute-done | bytes 262176 | tf_op jit(solution)/shard_map/ppermute | solution.py:437
  69.9 0.0 collective-permute-done.5.core_ref
  70.0 1.0 %gather_rows.1 = f32[1,1,4,256,256]{4,3,2,1,0:T(8,128)} custom-call(f32[256,256]{1,0:T(8,128)S(1)} %degrid_own.1.self_ref, f32[256,256]{1,0:T(8,128)S(1)} %collective-permute-done.5.core_ref, f32[256,256]{1,0:T(8,128)S(1)} %collective-permute-done.6.chip_ref, f32[256,256]{1,0:T(8,128)S(1)} %collective-permute-done.4.cross_ref), custom_call_target="tpu_custom_call" | custom-call | tf_op jit(solution)/shard_map/gather_rows/pallas_call | solution.py:404
  (27 shorter events, 0.1 us)
Async XLA Ops:
  0.0 5.0 %copy-start.11 = (bf16[4,256,256]{2,1,0:T(8,128)(2,1)S(1)}, bf16[4,256,256]{2,1,0:T(8,128)(2,1)}, u32[]{:S(2)}) copy-start(bf16[4,256,256]{2,1,0:T(8,128)(2,1)} %constant.14.clone.xtab_ref) | copy-start | bytes 1572868
  0.0 5.0 %copy-start.10 = (f32[128,8,256]{2,1,0:T(8,128)S(1)}, f32[128,8,256]{2,1,0:T(8,128)}, u32[]{:S(2)}) copy-start(f32[128,8,256]{2,1,0:T(8,128)} %constant.15.clone.xrot_ref) | copy-start | bytes 3145732
  0.0 5.0 %copy-start.4 = (f32[2,256,1024]{2,1,0:T(8,128)S(1)}, f32[2,256,1024]{2,1,0:T(8,128)}, u32[]{:S(2)}) copy-start(f32[2,256,1024]{2,1,0:T(8,128)} %facet_ref.3) | copy-start | bytes 6291460
  3.5 3.3 %copy-start.14 = (f32[128,512]{1,0:T(8,128)S(1)}, f32[128,512]{1,0:T(8,128)}, u32[]{:S(2)}) copy-start(f32[128,512]{1,0:T(8,128)} %get-tuple-element.18) | copy-start | bytes 786436
  3.5 10.9 %copy-start.9 = (bf16[16,2,256,256]{3,2,1,0:T(8,128)(2,1)S(1)}, bf16[16,2,256,256]{3,2,1,0:T(8,128)(2,1)}, u32[]{:S(2)}) copy-start(bf16[16,2,256,256]{3,2,1,0:T(8,128)(2,1)} %constant.16.clone.refs_3_) | copy-start | bytes 12582916
  3.5 10.9 %copy-start.12 = (f32[8,2048]{1,0:T(8,128)S(1)}, f32[8,2048]{1,0:T(8,128)}, u32[]{:S(2)}) copy-start(f32[8,2048]{1,0:T(8,128)} %constant.17.clone.refs_4_) | copy-start | bytes 196612
  3.5 10.9 %copy-start.13 = (f32[128,512]{1,0:T(8,128)S(1)}, f32[128,512]{1,0:T(8,128)}, u32[]{:S(2)}) copy-start(f32[128,512]{1,0:T(8,128)} %get-tuple-element.16.refs_0_) | copy-start | bytes 786436
  3.5 3.2 %collective-permute-start.2 = (f32[256,512]{1,0:T(8,128)}, f32[256,512]{1,0:T(8,128)S(1)}, u32[]{:S(2)}, u32[]{:S(2)}) collective-permute-start(f32[256,512]{1,0:T(8,128)} %get-tuple-element.17), channel_id=1, source_target_pairs={{0,1},{1,0},{2,3},{3,2},{4,5},{5,4},{6,7},{7,6},{8,9},{9,8},{10,11... | collective-permute-start | bytes 1572872 | tf_op jit(solution)/shard_map/ppermute | solution.py:425
  6.1 2.1 %collective-permute-start = (f32[256,512]{1,0:T(8,128)S(1)}, f32[256,512]{1,0:T(8,128)S(1)}, u32[]{:S(2)}, u32[]{:S(2)}) collective-permute-start(f32[256,512]{1,0:T(8,128)S(1)} %get-tuple-element.14), channel_id=1, source_target_pairs={{0,1},{1,0},{2,3},{3,2},{4,5},{5,4},{6,7},{7,6},{8,9},{9,8},{10,11... | collective-permute-start | bytes 1572872 | tf_op jit(solution)/shard_map/ppermute | solution.py:425
  6.8 7.6 %collective-permute-start.3 = (f32[128,512]{1,0:T(8,128)S(1)}, f32[128,512]{1,0:T(8,128)S(1)}, u32[]{:S(2)}, u32[]{:S(2)}) collective-permute-start(f32[128,512]{1,0:T(8,128)S(1)} %slice_add_fusion), channel_id=1, source_target_pairs={{0,2},{2,0},{1,3},{3,1},{4,6},{6,4},{5,7},{7,5},{8,10},{10,8},{9,1... | collective-permute-start | bytes 786440 | tf_op jit(solution)/shard_map/ppermute | solution.py:426
  8.2 11.8 %collective-permute-start.1 = (f32[128,512]{1,0:T(8,128)S(1)}, f32[128,512]{1,0:T(8,128)S(1)}, u32[]{:S(2)}, u32[]{:S(2)}) collective-permute-start(f32[128,512]{1,0:T(8,128)S(1)} %slice_add_fusion.1), channel_id=1, source_target_pairs={{0,2},{2,0},{1,3},{3,1},{4,6},{6,4},{5,7},{7,5},{8,10},{10,8},{9,1... | collective-permute-start | bytes 786440 | tf_op jit(solution)/shard_map/ppermute | solution.py:426
  20.0 14.3 %copy-start.7 = (s32[1,1,512,1]{2,3,1,0:T(1,128)S(1)}, s32[1,1,512,1]{2,3,1,0:T(1,128)}, u32[]{:S(2)}) copy-start(s32[1,1,512,1]{2,3,1,0:T(1,128)} %param.20) | copy-start | bytes 6148
  20.0 14.3 %copy-start.8 = (s32[1,1,512]{2,1,0:T(1,128)S(1)}, s32[1,1,512]{2,1,0:T(1,128)}, u32[]{:S(2)}) copy-start(s32[1,1,512]{2,1,0:T(1,128)} %wplanes_ref.9) | copy-start | bytes 6148
  20.0 30.0 %copy-start = (f32[2,64,512]{2,1,0:T(8,128)S(1)}, f32[2,64,512]{2,1,0:T(8,128)}, u32[]{:S(2)}) copy-start(f32[2,64,512]{2,1,0:T(8,128)} %constant.18.clone.screens_ref) | copy-start | bytes 786436
  20.0 30.0 %copy-start.1 = (f32[128,256]{1,0:T(8,128)S(1)}, f32[128,256]{1,0:T(8,128)}, u32[]{:S(2)}) copy-start(f32[128,256]{1,0:T(8,128)} %constant.20.clone.right_ref) | copy-start | bytes 393220
  20.0 30.0 %copy-start.2 = (f32[128,128]{1,0:T(8,128)S(1)}, f32[128,128]{1,0:T(8,128)}, u32[]{:S(2)}) copy-start(f32[128,128]{1,0:T(8,128)} %constant.19.clone.left_ref) | copy-start | bytes 196612
  20.0 30.0 %copy-start.3 = (s32[4,1,8]{2,1,0:T(1,128)S(1)}, s32[4,1,8]{2,1,0:T(1,128)}, u32[]{:S(2)}) copy-start(s32[4,1,8]{2,1,0:T(1,128)} %param.15) | copy-start | bytes 388
  22.9 28.8 %copy-start.5 = (s32[2,1,1,512,128]{4,3,2,1,0:T(8,128)S(1)}, s32[2,1,1,512,128]{4,3,2,1,0:T(8,128)}, u32[]{:S(2)}) copy-start(s32[2,1,1,512,128]{4,3,2,1,0:T(8,128)} %offsets_ref.7) | copy-start | bytes 1572868
  22.9 28.8 %copy-start.6 = (f32[2,1,1,512,128]{4,3,2,1,0:T(8,128)S(1)}, f32[2,1,1,512,128]{4,3,2,1,0:T(8,128)}, u32[]{:S(2)}) copy-start(f32[2,1,1,512,128]{4,3,2,1,0:T(8,128)} %frac_ref.7) | copy-start | bytes 1572868
  22.9 27.0 %all-to-all-start = ((f32[32,64,128]{2,1,0:T(8,128)}), f32[32,64,128]{2,1,0:T(8,128)S(1)}, u32[]{:S(2)}, u32[]{:S(2)}) async-start(f32[32,64,128]{2,1,0:T(8,128)} %y_sum_b.1), calls=%async_computation | async-start | bytes 2097152 | tf_op jit(solution)/shard_map/all_to_all | solution.py:431
  53.4 10.3 %collective-permute-start.4 = (f32[256,256]{1,0:T(8,128)S(1)}, f32[256,256]{1,0:T(8,128)S(1)}, u32[]{:S(2)}, u32[]{:S(2)}) collective-permute-start(f32[256,256]{1,0:T(8,128)S(1)} %degrid_cross.1), channel_id=1, source_target_pairs={{0,3},{3,0},{1,2},{2,1},{4,7},{7,4},{5,6},{6,5},{8,11},{11,8},{9,1... | collective-permute-start | bytes 786440 | tf_op jit(solution)/shard_map/ppermute | solution.py:436
  57.9 12.1 %collective-permute-start.6 = (f32[256,256]{1,0:T(8,128)S(1)}, f32[256,256]{1,0:T(8,128)S(1)}, u32[]{:S(2)}, u32[]{:S(2)}) collective-permute-start(f32[256,256]{1,0:T(8,128)S(1)} %degrid_chip.1), channel_id=1, source_target_pairs={{0,2},{2,0},{1,3},{3,1},{4,6},{6,4},{5,7},{7,5},{8,10},{10,8},{9,1... | collective-permute-start | bytes 786440 | tf_op jit(solution)/shard_map/ppermute | solution.py:437
  63.7 6.2 %collective-permute-start.5 = (f32[256,256]{1,0:T(8,128)S(1)}, f32[256,256]{1,0:T(8,128)S(1)}, u32[]{:S(2)}, u32[]{:S(2)}) collective-permute-start(f32[256,256]{1,0:T(8,128)S(1)} %degrid_core.1), channel_id=1, source_target_pairs={{0,1},{1,0},{2,3},{3,2},{4,5},{5,4},{6,7},{7,6},{8,9},{9,8},{10,11... | collective-permute-start | bytes 786440 | tf_op jit(solution)/shard_map/ppermute | solution.py:439

commit v4 on v3

--- a/solution.py
+++ b/solution.py
@@ -96,6 +96,12 @@
 
 def dot(a, b):
     return jnp.dot(a, b, preferred_element_type=F32)
+
+
+def dot3(a, b):
+    a_hi, a_lo = split(a)
+    b_hi, b_lo = split(b)
+    return dot(jnp.concatenate([a_hi, a_lo, a_hi], 1), jnp.concatenate([b_hi, b_hi, b_lo], 0))
 
 
 def x_kernel(facet_ref, xtab_ref, xrot_ref, send_ref, k0_ref, k1_ref, rot_ref, *scratch, half):
@@ -171,7 +177,8 @@
     if half == 0:
         kept_ref, near_ref, far_ref, ytab_ref, yrot_ref, out_ref, lhs_ref = refs
     else:
-        kept_ref, near_ref, far_ref, ytab_ref, yrot_ref, first_ref, out_ref, lhs_ref = refs
+        kept_ref, near_ref, far_ref, ytab_ref, yrot_ref, first_ref, sent_ref, lhs_ref, out_ref, sems = refs
+    copies = []
 
     hi, lo = split(kept_ref[...] + near_ref[2 * SUB :] + far_ref[...])
     lhs = []
@@ -202,23 +209,30 @@
             even, odd = even + first_ref[2 * w], odd + first_ref[2 * w + 1]
         out_ref[2 * w] = even
         out_ref[2 * w + 1] = odd
+        if half == 1 and w % 4 == 3:
+            columns = pl.ds(2 * w - 6, 8)
+            copies.append(pltpu.make_async_copy(out_ref.at[columns], sent_ref.at[columns], sems.at[w // 4]))
+            copies[-1].start()
+    for copy in copies:
+        copy.wait()
 
 
 def y_sum(half, kept, received, far, ytab, yrot, *first):
     vmem = pl.BlockSpec(memory_space=pltpu.VMEM)
+    sending = [pltpu.VMEM((NCOL, SUB, 2 * SUB), F32), pltpu.SemaphoreType.DMA((NCOL // 8,))]
     return pl.pallas_call(
         functools.partial(y_kernel, half=half),
         in_specs=[vmem] * (5 + len(first)),
-        out_specs=vmem,
+        out_specs=vmem if half == 0 else pl.BlockSpec(memory_space=pl.ANY),
         out_shape=jax.ShapeDtypeStruct((NCOL, SUB, 2 * SUB), F32),
-        scratch_shapes=[pltpu.VMEM((2 * 128, 3 * YBLK), BF16)],
+        scratch_shapes=[pltpu.VMEM((2 * 128, 3 * YBLK), BF16)] + (sending if half == 1 else []),
         compiler_params=pltpu.CompilerParams(vmem_limit_bytes=VMEM_LIMIT),
         cost_estimate=pl.CostEstimate(flops=3_000_000_000, bytes_accessed=6_000_000, transcendentals=0),
         name="y_sum_" + "ab"[half],
     )(kept, received, far, ytab, yrot, *first)
 
 
-TAPER = math.sqrt(0.5 * math.log2(math.e)) / 1.6
+TAPER = -0.5 * math.log2(math.e) / 1.6**2
 STEP = 32
 SPAN = ROWS + N_VIS * (NW + STEP)
 ENDS = SPAN + 8
@@ -297,10 +311,10 @@
     gim = jnp.concatenate([turned[SUB:]] * NW, 1)
     hre = gre * screens_ref[0] - gim * screens_ref[1]
     him = gre * screens_ref[1] + gim * screens_ref[0]
-    along = jnp.dot(left_ref[...], jnp.concatenate([hre, him], 0), precision=HIGHEST, preferred_element_type=F32)
+    along = dot3(left_ref[...], jnp.concatenate([hre, him], 0))
     first = lax.broadcasted_iota(jnp.int32, (128, 128), 1) < 64
     for pair in range(NW // 2):
-        m = jnp.dot(along[:, pair * 128 : (pair + 1) * 128], right_ref[...], precision=HIGHEST, preferred_element_type=F32)
+        m = dot3(along[:, pair * 128 : (pair + 1) * 128], right_ref[...])
         re = m[:SUB, :128] + m[SUB:, 128:]
         im = m[SUB:, :128] - m[:SUB, 128:]
         both = jnp.concatenate([re, im], 0)
@@ -332,10 +346,9 @@
 
     def taps(axis, n):
         offset = jnp.broadcast_to(offsets_ref[axis, 0, 0, pl.ds(n, 1), :], (8, CH))
-        shift = (jnp.broadcast_to(frac_ref[axis, 0, 0, pl.ds(n, 1), :], (8, CH)) + 3.5) * TAPER
-        step = ((cell - offset) & 7).astype(F32)
-        d = step * TAPER - shift
-        return jnp.exp2(-(d * d)), (offset - ahead) >> 3
+        shift = jnp.broadcast_to(frac_ref[axis, 0, 0, pl.ds(n, 1), :], (8, CH)) + 3.5
+        d = ((cell - offset) & 7).astype(F32) - shift
+        return jnp.exp2(d * d * TAPER), (offset - ahead) >> 3
 
     def body(group, carry):
         base = group * STEP

time: 70.3 us -> 70.5 us (level); the launches traced: 70.9 us -> 70 us
  starting transfers between devices: 23.1 us -> 21.1 us
  Pallas kernels: 27 us -> 28.3 us
    ppermute x1, starting transfers between devices: 4.17 us -> 1.65 us  [on_device(): from_chip = lax.ppermute(to_chip, 'vis', TO_CHIP)]
    pallas_call x4, Pallas kernels: 6.54 us -> 8.4 us  [degrid(): pl.pallas_call(functools.partial(degrid_kernel, part=part), in_specs=[sme...]
    ppermute x1, starting transfers between devices: 2.33 us -> 3.32 us  [on_device(): from_cross = lax.ppermute(to_cross, 'vis', TO_CROSS)]
  transfers between devices with their start and end apart: 8 -> 8, of which waited for: 5 -> 5; matrix products, arithmetic and copies ran while one was open for 0% -> 0% of each run, Pallas kernels for 23% -> 26%
where the time goes in v4:
time: 70.5 us; the launch traced here: 70 us
  Pallas kernels  28.3 us (40%)
  starting transfers between devices  21.1 us (30%)
  waiting for transfers between devices  19.7 us (28%)
  between operations  0.88 us (1%)
    all_to_all x1, starting transfers between devices, on_device(): lax.all_to_all(blocks, 'facet', split_axis=0, concat_axis=0, tiled=True)  10.7 us
    ppermute x2, waiting for transfers between devices, on_device(): far = lax.ppermute(k0 + received[:2 * SUB], 'vis', TO_CHIP)  8.59 us
    pallas_call x1, Pallas kernels, order_rows(): pl.pallas_call(order_kernel, in_specs=[smem] * 3, out_specs=smem, out_sha...  8.45 us
    pallas_call x4, Pallas kernels, degrid(): pl.pallas_call(functools.partial(degrid_kernel, part=part), in_specs=[sme...  8.4 us
    all_to_all x1, waiting for transfers between devices, on_device(): lax.all_to_all(blocks, 'facet', split_axis=0, concat_axis=0, tiled=True)  7.17 us
    pallas_call x2, Pallas kernels, y_sum(): pl.pallas_call(functools.partial(y_kernel, half=half), in_specs=[vmem] *...  4.57 us
    pallas_call x2, Pallas kernels, x_sum(): pl.pallas_call(functools.partial(x_kernel, half=half), in_specs=[pl.Block...  4.51 us
    ppermute x1, waiting for transfers between devices, on_device(): from_chip = lax.ppermute(to_chip, 'vis', TO_CHIP)  3.34 us
  transfers between devices with their start and end apart: 8, of which 5 were waited for; matrix products, arithmetic and copies ran while one was open for 0% of the time, Pallas kernels for 26%

profile of v4, /device:TPU:1, one launch (start us, length us, event | category | flops | bytes accessed | tf_op | source)
XLA Modules:
  0.0 70.0 jit_solution(882075156698435065)
XLA Ops:
  0.0 3.4 %x_sum_a.1 = (f32[256,512]{1,0:T(8,128)}, f32[128,512]{1,0:T(8,128)}, f32[128,512]{1,0:T(8,128)}) custom-call(f32[2,256,1024]{2,1,0:T(8,128)} %facet_ref.3, bf16[4,256,256]{2,1,0:T(8,128)(2,1)} %constant.14.clone.xtab_ref, f32[128,8,256]{2,1,0:T(8,128)} %constant.15.clone.xrot_ref), custom_call_target="tpu_custom_call" | custom-call | flops 2000000000 | bytes 2000000 | tf_op jit(solution)/shard_map/x_sum_a/pallas_call | solution.py:164
  3.5 0.0 copy-start.9
  3.5 0.0 copy-start.12
  3.5 1.5 %collective-permute-start.2 = (f32[256,512]{1,0:T(8,128)}, f32[256,512]{1,0:T(8,128)S(1)}, u32[]{:S(2)}, u32[]{:S(2)}) collective-permute-start(f32[256,512]{1,0:T(8,128)} %get-tuple-element.17), channel_id=1, source_target_pairs={{0,1},{1,0},{2,3},{3,2},{4,5},{5,4},{6,7},{7,6},{8,9},{9,8},{10,11... | collective-permute-start | bytes 1572872 | tf_op jit(solution)/shard_map/ppermute | solution.py:438
  5.0 1.1 %x_sum_b.1 = (f32[256,512]{1,0:T(8,128)S(1)}, f32[128,512]{1,0:T(8,128)S(1)}, f32[128,512]{1,0:T(8,128)S(1)}) custom-call(f32[2,256,1024]{2,1,0:T(8,128)S(1)} %copy-done.4, bf16[4,256,256]{2,1,0:T(8,128)(2,1)S(1)} %copy-done.11, f32[128,8,256]{2,1,0:T(8,128)S(1)} %copy-done.10), custom_call_target="tpu_custom_call" | custom-call | flops 2000000000 | bytes 2000000 | tf_op jit(solution)/shard_map/x_sum_b/pallas_call | solution.py:164
  6.1 0.1 collective-permute-start
  6.2 0.6 collective-permute-done.2.refs_1_
  6.8 1.4 %collective-permute-start.3 = (f32[128,512]{1,0:T(8,128)S(1)}, f32[128,512]{1,0:T(8,128)S(1)}, u32[]{:S(2)}, u32[]{:S(2)}) collective-permute-start(f32[128,512]{1,0:T(8,128)S(1)} %slice_add_fusion), channel_id=1, source_target_pairs={{0,2},{2,0},{1,3},{3,1},{4,6},{6,4},{5,7},{7,5},{8,10},{10,8},{9,1... | collective-permute-start | bytes 786440 | tf_op jit(solution)/shard_map/ppermute | solution.py:439
  8.2 0.0 collective-permute-done.refs_1_
  8.2 1.3 %collective-permute-start.1 = (f32[128,512]{1,0:T(8,128)S(1)}, f32[128,512]{1,0:T(8,128)S(1)}, u32[]{:S(2)}, u32[]{:S(2)}) collective-permute-start(f32[128,512]{1,0:T(8,128)S(1)} %slice_add_fusion.1), channel_id=1, source_target_pairs={{0,2},{2,0},{1,3},{3,1},{4,6},{6,4},{5,7},{7,5},{8,10},{10,8},{9,1... | collective-permute-start | bytes 786440 | tf_op jit(solution)/shard_map/ppermute | solution.py:439
  9.5 4.9 %collective-permute-done.3.refs_2_ = f32[128,512]{1,0:T(8,128)S(1)} collective-permute-done((f32[128,512]{1,0:T(8,128)S(1)}, f32[128,512]{1,0:T(8,128)S(1)}, u32[]{:S(2)}, u32[]{:S(2)}) %collective-permute-start.3) | collective-permute-done | bytes 262176 | tf_op jit(solution)/shard_map/ppermute | solution.py:439
  14.4 1.9 %y_sum_a.1.refs_5_ = f32[32,64,128]{2,1,0:T(8,128)S(1)} custom-call(f32[128,512]{1,0:T(8,128)S(1)} %copy-done.13, f32[256,512]{1,0:T(8,128)S(1)} %collective-permute-done.2.refs_1_, f32[128,512]{1,0:T(8,128)S(1)} %collective-permute-done.3.refs_2_, bf16[16,2,256,256]{3,2,1,0:T(8,128)(2,1)S(1)} %copy-done.9, f32[8,2048]{1,0:T(8,128)S(1)} %copy-done.12), custom_call_target="tpu_custom_call" | custom-call | flops 3000000000 | bytes 6000000 | tf_op jit(solution)/shard_map/y_sum_a/pallas_call | solution.py:223
  16.3 3.7 %collective-permute-done.1.refs_2_ = f32[128,512]{1,0:T(8,128)S(1)} collective-permute-done((f32[128,512]{1,0:T(8,128)S(1)}, f32[128,512]{1,0:T(8,128)S(1)}, u32[]{:S(2)}, u32[]{:S(2)}) %collective-permute-start.1) | collective-permute-done | bytes 262176 | tf_op jit(solution)/shard_map/ppermute | solution.py:439
  20.0 0.0 copy-start.2
  20.0 0.0 copy-start.3
  20.0 2.7 %y_sum_b.1 = f32[32,64,128]{2,1,0:T(8,128)} custom-call(f32[128,512]{1,0:T(8,128)S(1)} %get-tuple-element.13.refs_0_, f32[256,512]{1,0:T(8,128)S(1)} %collective-permute-done.refs_1_, f32[128,512]{1,0:T(8,128)S(1)} %collective-permute-done.1.refs_2_, bf16[16,2,256,256]{3,2,1,0:T(8,128)(2,1)S(1)} %copy-done.9, f32[8,2048]{1,0:T(8,128)S(1)} %copy-done.12, ...), custom_call_target="tpu_custom_call" | custom-call | flops 3000000000 | bytes 6000000 | tf_op jit(solution)/shard_map/y_sum_b/pallas_call | solution.py:223
  22.7 0.0 copy-start.5
  22.7 0.0 copy-start.6
  22.7 10.7 %all-to-all-start = ((f32[32,64,128]{2,1,0:T(8,128)}), f32[32,64,128]{2,1,0:T(8,128)S(1)}, u32[]{:S(2)}, u32[]{:S(2)}) async-start(f32[32,64,128]{2,1,0:T(8,128)} %y_sum_b.1), calls=%async_computation | async-start | bytes 2097152 | tf_op jit(solution)/shard_map/all_to_all | solution.py:444
  34.2 8.4 %order_rows.1.order_ref = s32[688]{0:T(1024)S(1)} custom-call(s32[1,1]{1,0:T(1,128)S(6)} %copy.15.counts_ref, s32[1,1,512]{2,1,0:T(1,128)S(1)} %copy-done.8, s32[1,1,512]{2,1,0:T(1,128)S(1)} %bitcast.3), custom_call_target="tpu_custom_call" | custom-call | flops 20000000 | bytes 20000000 | tf_op jit(solution)/shard_map/order_rows/pallas_call | solution.py:292
  42.6 7.2 %all-to-all-done.blocks_ref = f32[32,64,128]{2,1,0:T(8,128)S(1)} async-done(((f32[32,64,128]{2,1,0:T(8,128)}), f32[32,64,128]{2,1,0:T(8,128)S(1)}, u32[]{:S(2)}, u32[]{:S(2)}) %all-to-all-start) | async-done | bytes 1048608 | tf_op jit(solution)/shard_map/all_to_all | solution.py:444
  49.8 1.3 %make_planes.1.planes_ref = bf16[8,128,256]{2,1,0:T(8,128)(2,1)S(1)} custom-call(s32[4,8]{1,0:T(4,128)S(1)} %bitcast.2, f32[32,64,128]{2,1,0:T(8,128)S(1)} %all-to-all-done.blocks_ref, f32[2,64,512]{2,1,0:T(8,128)S(1)} %copy-done, f32[128,128]{1,0:T(8,128)S(1)} %copy-done.2, f32[128,256]{1,0:T(8,128)S(1)} %copy-done.1), custom_call_target="tpu_custom_call" | custom-call | tf_op jit(solution)/shard_map/make_planes/pallas_call | solution.py:330
  51.2 1.6 %degrid_cross.1 = f32[256,256]{1,0:T(8,128)S(1)} custom-call(s32[688]{0:T(1024)S(1)} %order_rows.1.order_ref, s32[1,1,512]{2,1,0:T(1,128)S(1)} %copy-done.8, bf16[8,128,256]{2,1,0:T(8,128)(2,1)S(1)} %make_planes.1.planes_ref, s32[2,1,1,512,128]{4,3,2,1,0:T(8,128)S(1)} %copy-done.5, f32[2,1,1,512,128]{4,3,2,1,0:T(8,128)S(1)} %copy-done.6), custom_call_target="tpu_custom_call" | custom-call | flops 2500000000 | bytes 2000000 | tf_op jit(solution)/shard_map/degrid_cross/pallas_call | solution.py:392
  52.8 3.3 %collective-permute-start.4 = (f32[256,256]{1,0:T(8,128)S(1)}, f32[256,256]{1,0:T(8,128)S(1)}, u32[]{:S(2)}, u32[]{:S(2)}) collective-permute-start(f32[256,256]{1,0:T(8,128)S(1)} %degrid_cross.1), channel_id=1, source_target_pairs={{0,3},{3,0},{1,2},{2,1},{4,7},{7,4},{5,6},{6,5},{8,11},{11,8},{9,1... | collective-permute-start | bytes 786440 | tf_op jit(solution)/shard_map/ppermute | solution.py:449
  56.1 3.1 %degrid_chip.1 = f32[256,256]{1,0:T(8,128)S(1)} custom-call(s32[688]{0:T(1024)S(1)} %order_rows.1.order_ref, s32[1,1,512]{2,1,0:T(1,128)S(1)} %copy-done.8, bf16[8,128,256]{2,1,0:T(8,128)(2,1)S(1)} %make_planes.1.planes_ref, s32[2,1,1,512,128]{4,3,2,1,0:T(8,128)S(1)} %copy-done.5, f32[2,1,1,512,128]{4,3,2,1,0:T(8,128)S(1)} %copy-done.6), custom_call_target="tpu_custom_call" | custom-call | flops 2500000000 | bytes 2000000 | tf_op jit(solution)/shard_map/degrid_chip/pallas_call | solution.py:392
  59.2 1.7 %collective-permute-start.6 = (f32[256,256]{1,0:T(8,128)S(1)}, f32[256,256]{1,0:T(8,128)S(1)}, u32[]{:S(2)}, u32[]{:S(2)}) collective-permute-start(f32[256,256]{1,0:T(8,128)S(1)} %degrid_chip.1), channel_id=1, source_target_pairs={{0,2},{2,0},{1,3},{3,1},{4,6},{6,4},{5,7},{7,5},{8,10},{10,8},{9,1... | collective-permute-start | bytes 786440 | tf_op jit(solution)/shard_map/ppermute | solution.py:450
  60.9 2.6 %degrid_core.1 = f32[256,256]{1,0:T(8,128)S(1)} custom-call(s32[688]{0:T(1024)S(1)} %order_rows.1.order_ref, s32[1,1,512]{2,1,0:T(1,128)S(1)} %copy-done.8, bf16[8,128,256]{2,1,0:T(8,128)(2,1)S(1)} %make_planes.1.planes_ref, s32[2,1,1,512,128]{4,3,2,1,0:T(8,128)S(1)} %copy-done.5, f32[2,1,1,512,128]{4,3,2,1,0:T(8,128)S(1)} %copy-done.6), custom_call_target="tpu_custom_call" | custom-call | flops 2500000000 | bytes 2000000 | tf_op jit(solution)/shard_map/degrid_core/pallas_call | solution.py:392
  63.4 0.0 collective-permute-done.4.cross_ref
  63.4 1.1 %collective-permute-start.5 = (f32[256,256]{1,0:T(8,128)S(1)}, f32[256,256]{1,0:T(8,128)S(1)}, u32[]{:S(2)}, u32[]{:S(2)}) collective-permute-start(f32[256,256]{1,0:T(8,128)S(1)} %degrid_core.1), channel_id=1, source_target_pairs={{0,1},{1,0},{2,3},{3,2},{4,5},{5,4},{6,7},{7,6},{8,9},{9,8},{10,11... | collective-permute-start | bytes 786440 | tf_op jit(solution)/shard_map/ppermute | solution.py:452
  64.5 1.1 %degrid_own.1.self_ref = f32[256,256]{1,0:T(8,128)S(1)} custom-call(s32[688]{0:T(1024)S(1)} %order_rows.1.order_ref, s32[1,1,512]{2,1,0:T(1,128)S(1)} %copy-done.8, bf16[8,128,256]{2,1,0:T(8,128)(2,1)S(1)} %make_planes.1.planes_ref, s32[2,1,1,512,128]{4,3,2,1,0:T(8,128)S(1)} %copy-done.5, f32[2,1,1,512,128]{4,3,2,1,0:T(8,128)S(1)} %copy-done.6), custom_call_target="tpu_custom_call" | custom-call | flops 2500000000 | bytes 2000000 | tf_op jit(solution)/shard_map/degrid_own/pallas_call | solution.py:392
  65.7 3.3 %collective-permute-done.6.chip_ref = f32[256,256]{1,0:T(8,128)S(1)} collective-permute-done((f32[256,256]{1,0:T(8,128)S(1)}, f32[256,256]{1,0:T(8,128)S(1)}, u32[]{:S(2)}, u32[]{:S(2)}) %collective-permute-start.6) | collective-permute-done | bytes 262176 | tf_op jit(solution)/shard_map/ppermute | solution.py:450
  69.0 1.0 %gather_rows.1 = f32[1,1,4,256,256]{4,3,2,1,0:T(8,128)} custom-call(f32[256,256]{1,0:T(8,128)S(1)} %degrid_own.1.self_ref, f32[256,256]{1,0:T(8,128)S(1)} %collective-permute-done.5.core_ref, f32[256,256]{1,0:T(8,128)S(1)} %collective-permute-done.6.chip_ref, f32[256,256]{1,0:T(8,128)S(1)} %collective-permute-done.4.cross_ref), custom_call_target="tpu_custom_call" | custom-call | tf_op jit(solution)/shard_map/gather_rows/pallas_call | solution.py:417
  (27 shorter events, 0.1 us)
Async XLA Ops:
  0.0 5.0 %copy-start.11 = (bf16[4,256,256]{2,1,0:T(8,128)(2,1)S(1)}, bf16[4,256,256]{2,1,0:T(8,128)(2,1)}, u32[]{:S(2)}) copy-start(bf16[4,256,256]{2,1,0:T(8,128)(2,1)} %constant.14.clone.xtab_ref) | copy-start | bytes 1572868
  0.0 5.0 %copy-start.10 = (f32[128,8,256]{2,1,0:T(8,128)S(1)}, f32[128,8,256]{2,1,0:T(8,128)}, u32[]{:S(2)}) copy-start(f32[128,8,256]{2,1,0:T(8,128)} %constant.15.clone.xrot_ref) | copy-start | bytes 3145732
  0.0 5.0 %copy-start.4 = (f32[2,256,1024]{2,1,0:T(8,128)S(1)}, f32[2,256,1024]{2,1,0:T(8,128)}, u32[]{:S(2)}) copy-start(f32[2,256,1024]{2,1,0:T(8,128)} %facet_ref.3) | copy-start | bytes 6291460
  3.5 3.3 %copy-start.14 = (f32[128,512]{1,0:T(8,128)S(1)}, f32[128,512]{1,0:T(8,128)}, u32[]{:S(2)}) copy-start(f32[128,512]{1,0:T(8,128)} %get-tuple-element.18) | copy-start | bytes 786436
  3.5 10.9 %copy-start.9 = (bf16[16,2,256,256]{3,2,1,0:T(8,128)(2,1)S(1)}, bf16[16,2,256,256]{3,2,1,0:T(8,128)(2,1)}, u32[]{:S(2)}) copy-start(bf16[16,2,256,256]{3,2,1,0:T(8,128)(2,1)} %constant.16.clone.refs_3_) | copy-start | bytes 12582916
  3.5 10.9 %copy-start.12 = (f32[8,2048]{1,0:T(8,128)S(1)}, f32[8,2048]{1,0:T(8,128)}, u32[]{:S(2)}) copy-start(f32[8,2048]{1,0:T(8,128)} %constant.17.clone.refs_4_) | copy-start | bytes 196612
  3.5 10.9 %copy-start.13 = (f32[128,512]{1,0:T(8,128)S(1)}, f32[128,512]{1,0:T(8,128)}, u32[]{:S(2)}) copy-start(f32[128,512]{1,0:T(8,128)} %get-tuple-element.16.refs_0_) | copy-start | bytes 786436
  3.5 3.2 %collective-permute-start.2 = (f32[256,512]{1,0:T(8,128)}, f32[256,512]{1,0:T(8,128)S(1)}, u32[]{:S(2)}, u32[]{:S(2)}) collective-permute-start(f32[256,512]{1,0:T(8,128)} %get-tuple-element.17), channel_id=1, source_target_pairs={{0,1},{1,0},{2,3},{3,2},{4,5},{5,4},{6,7},{7,6},{8,9},{9,8},{10,11... | collective-permute-start | bytes 1572872 | tf_op jit(solution)/shard_map/ppermute | solution.py:438
  6.1 2.1 %collective-permute-start = (f32[256,512]{1,0:T(8,128)S(1)}, f32[256,512]{1,0:T(8,128)S(1)}, u32[]{:S(2)}, u32[]{:S(2)}) collective-permute-start(f32[256,512]{1,0:T(8,128)S(1)} %get-tuple-element.14), channel_id=1, source_target_pairs={{0,1},{1,0},{2,3},{3,2},{4,5},{5,4},{6,7},{7,6},{8,9},{9,8},{10,11... | collective-permute-start | bytes 1572872 | tf_op jit(solution)/shard_map/ppermute | solution.py:438
  6.8 7.6 %collective-permute-start.3 = (f32[128,512]{1,0:T(8,128)S(1)}, f32[128,512]{1,0:T(8,128)S(1)}, u32[]{:S(2)}, u32[]{:S(2)}) collective-permute-start(f32[128,512]{1,0:T(8,128)S(1)} %slice_add_fusion), channel_id=1, source_target_pairs={{0,2},{2,0},{1,3},{3,1},{4,6},{6,4},{5,7},{7,5},{8,10},{10,8},{9,1... | collective-permute-start | bytes 786440 | tf_op jit(solution)/shard_map/ppermute | solution.py:439
  8.2 11.8 %collective-permute-start.1 = (f32[128,512]{1,0:T(8,128)S(1)}, f32[128,512]{1,0:T(8,128)S(1)}, u32[]{:S(2)}, u32[]{:S(2)}) collective-permute-start(f32[128,512]{1,0:T(8,128)S(1)} %slice_add_fusion.1), channel_id=1, source_target_pairs={{0,2},{2,0},{1,3},{3,1},{4,6},{6,4},{5,7},{7,5},{8,10},{10,8},{9,1... | collective-permute-start | bytes 786440 | tf_op jit(solution)/shard_map/ppermute | solution.py:439
  20.0 14.1 %copy-start.7 = (s32[1,1,512,1]{2,3,1,0:T(1,128)S(1)}, s32[1,1,512,1]{2,3,1,0:T(1,128)}, u32[]{:S(2)}) copy-start(s32[1,1,512,1]{2,3,1,0:T(1,128)} %param.20) | copy-start | bytes 6148
  20.0 14.1 %copy-start.8 = (s32[1,1,512]{2,1,0:T(1,128)S(1)}, s32[1,1,512]{2,1,0:T(1,128)}, u32[]{:S(2)}) copy-start(s32[1,1,512]{2,1,0:T(1,128)} %wplanes_ref.9) | copy-start | bytes 6148
  20.0 29.8 %copy-start = (f32[2,64,512]{2,1,0:T(8,128)S(1)}, f32[2,64,512]{2,1,0:T(8,128)}, u32[]{:S(2)}) copy-start(f32[2,64,512]{2,1,0:T(8,128)} %constant.18.clone.screens_ref) | copy-start | bytes 786436
  20.0 29.8 %copy-start.1 = (f32[128,256]{1,0:T(8,128)S(1)}, f32[128,256]{1,0:T(8,128)}, u32[]{:S(2)}) copy-start(f32[128,256]{1,0:T(8,128)} %constant.20.clone.right_ref) | copy-start | bytes 393220
  20.0 29.8 %copy-start.2 = (f32[128,128]{1,0:T(8,128)S(1)}, f32[128,128]{1,0:T(8,128)}, u32[]{:S(2)}) copy-start(f32[128,128]{1,0:T(8,128)} %constant.19.clone.left_ref) | copy-start | bytes 196612
  20.0 29.8 %copy-start.3 = (s32[4,1,8]{2,1,0:T(1,128)S(1)}, s32[4,1,8]{2,1,0:T(1,128)}, u32[]{:S(2)}) copy-start(s32[4,1,8]{2,1,0:T(1,128)} %param.15) | copy-start | bytes 388
  22.7 28.4 %copy-start.5 = (s32[2,1,1,512,128]{4,3,2,1,0:T(8,128)S(1)}, s32[2,1,1,512,128]{4,3,2,1,0:T(8,128)}, u32[]{:S(2)}) copy-start(s32[2,1,1,512,128]{4,3,2,1,0:T(8,128)} %offsets_ref.7) | copy-start | bytes 1572868
  22.7 28.4 %copy-start.6 = (f32[2,1,1,512,128]{4,3,2,1,0:T(8,128)S(1)}, f32[2,1,1,512,128]{4,3,2,1,0:T(8,128)}, u32[]{:S(2)}) copy-start(f32[2,1,1,512,128]{4,3,2,1,0:T(8,128)} %frac_ref.7) | copy-start | bytes 1572868
  22.7 27.0 %all-to-all-start = ((f32[32,64,128]{2,1,0:T(8,128)}), f32[32,64,128]{2,1,0:T(8,128)S(1)}, u32[]{:S(2)}, u32[]{:S(2)}) async-start(f32[32,64,128]{2,1,0:T(8,128)} %y_sum_b.1), calls=%async_computation | async-start | bytes 2097152 | tf_op jit(solution)/shard_map/all_to_all | solution.py:444
  52.8 10.6 %collective-permute-start.4 = (f32[256,256]{1,0:T(8,128)S(1)}, f32[256,256]{1,0:T(8,128)S(1)}, u32[]{:S(2)}, u32[]{:S(2)}) collective-permute-start(f32[256,256]{1,0:T(8,128)S(1)} %degrid_cross.1), channel_id=1, source_target_pairs={{0,3},{3,0},{1,2},{2,1},{4,7},{7,4},{5,6},{6,5},{8,11},{11,8},{9,1... | collective-permute-start | bytes 786440 | tf_op jit(solution)/shard_map/ppermute | solution.py:449
  59.2 9.8 %collective-permute-start.6 = (f32[256,256]{1,0:T(8,128)S(1)}, f32[256,256]{1,0:T(8,128)S(1)}, u32[]{:S(2)}, u32[]{:S(2)}) collective-permute-start(f32[256,256]{1,0:T(8,128)S(1)} %degrid_chip.1), channel_id=1, source_target_pairs={{0,2},{2,0},{1,3},{3,1},{4,6},{6,4},{5,7},{7,5},{8,10},{10,8},{9,1... | collective-permute-start | bytes 786440 | tf_op jit(solution)/shard_map/ppermute | solution.py:450
  63.4 5.6 %collective-permute-start.5 = (f32[256,256]{1,0:T(8,128)S(1)}, f32[256,256]{1,0:T(8,128)S(1)}, u32[]{:S(2)}, u32[]{:S(2)}) collective-permute-start(f32[256,256]{1,0:T(8,128)S(1)} %degrid_core.1), channel_id=1, source_target_pairs={{0,1},{1,0},{2,3},{3,2},{4,5},{5,4},{6,7},{7,6},{8,9},{9,8},{10,11... | collective-permute-start | bytes 786440 | tf_op jit(solution)/shard_map/ppermute | solution.py:452
